TPU v7x, 32 devices: a whole 2x2x4 slice. The times are simulated.
32 devices in a mesh: dp: 8 (over y, x, core), tensor: 4 (over z).
Axes of the slice: x: 2, y: 2, z: 4, core: 2. Of those that a mesh axis runs over, the one named last changes fastest.
Arguments:
- tokens: bfloat16 [16384, 768], P('dp'), may hold values from -6 to 6
- cotangent: bfloat16 [16384, 768], P(('dp', 'tensor')), may hold values from -6 to 6
- segment_ids: int32 [32, 512], P('dp'), may hold values from 0 to 7, never falling along the last dimension, each value on 1 to 128 neighbouring positions
- input_weight: float32 [3, 768, 768], P(None, 'dp', 'tensor'), may hold values from -0.21875 to 0.21875
- input_first: float32 [3, 768, 768], P(None, 'dp', 'tensor'), as said below
- input_second: float32 [3, 768, 768], P(None, 'dp', 'tensor'), may hold values from 16384 to 65536
- output_weight: float32 [768, 768], P('tensor', 'dp'), may hold values from -1 to 1
- output_first: float32 [768, 768], P('tensor', 'dp'), as said below
- output_second: float32 [768, 768], P('tensor', 'dp'), may hold values from 655 to 2621
- up_weight: float32 [768, 3072], P('dp', 'tensor'), may hold values from -0.21875 to 0.21875
- up_first: float32 [768, 3072], P('dp', 'tensor'), as said below
- up_second: float32 [768, 3072], P('dp', 'tensor'), may hold values from 1489 to 5957
- down_weight: float32 [3072, 768], P('tensor', 'dp'), may hold values from -0.109375 to 0.109375
- down_first: float32 [3072, 768], P('tensor', 'dp'), as said below
- down_second: float32 [3072, 768], P('tensor', 'dp'), may hold values from 5461 to 21845
- inner_bias: float32 [6, 768], P(None, 'tensor'), may hold values from -3 to 3
- inner_first: float32 [6, 768], P(None, 'tensor'), as said below
- inner_second: float32 [6, 768], P(None, 'tensor'), may hold values from 16384 to 65536
- vectors: float32 [6, 768], replicated, may hold values from -1 to 2, as said below
- vector_first: float32 [6, 768], replicated, as said below
- vector_second: float32 [6, 768], replicated, may hold values from 16384 to 65536
Outputs:
- block_out: bfloat16 [16384, 768], P(('dp', 'tensor'))
- token_grad: float32 [16384, 768], P(('dp', 'tensor'))
- new_input_weight: float32 [3, 768, 768], P(None, 'dp', 'tensor')
- new_input_first: float32 [3, 768, 768], P(None, 'dp', 'tensor')
- new_input_second: float32 [3, 768, 768], P(None, 'dp', 'tensor')
- new_output_weight: float32 [768, 768], P('tensor', 'dp')
- new_output_first: float32 [768, 768], P('tensor', 'dp')
- new_output_second: float32 [768, 768], P('tensor', 'dp')
- new_up_weight: float32 [768, 3072], P('dp', 'tensor')
- new_up_first: float32 [768, 3072], P('dp', 'tensor')
- new_up_second: float32 [768, 3072], P('dp', 'tensor')
- new_down_weight: float32 [3072, 768], P('tensor', 'dp')
- new_down_first: float32 [3072, 768], P('tensor', 'dp')
- new_down_second: float32 [3072, 768], P('tensor', 'dp')
- new_inner_bias: float32 [6, 768], P(None, 'tensor')
- new_inner_first: float32 [6, 768], P(None, 'tensor')
- new_inner_second: float32 [6, 768], P(None, 'tensor')
- new_vectors: float32 [6, 768], replicated
- new_vector_first: float32 [6, 768], replicated
- new_vector_second: float32 [6, 768], replicated
Inputs may be any that keep to these rules, and one draw needn't show every extreme that they name: `segment_ids`: along each packed row the numbers never fall; each of the 8 segments covers 1 to 128 slots, and one covers exactly 128. `input_first`: both signs occur. `output_first`: both signs occur. `up_first`: both signs occur. `down_first`: both signs occur. `inner_first`: both signs occur. `vector_first`: both signs occur. `vectors`: rows 1 and 4 are gains near one, the others biases.
All inputs are finite; a program needn't handle non-finite values.
Results may differ from a plain program's by a relative error of at most 0.019.
Values may be sent and summed in bfloat16 or wider, within the bound.
A program may use at most 128 MiB of HBM per device.

v0:
```python
from functools import partial
import math

import jax
import jax.numpy as jnp
from jax import lax
from jax.sharding import PartitionSpec as P

DH = 64
STEP = 5


NORM_EPS = 1e-05
NEG_FILL = -1e30
BETA = 0.5
ADAM_EPS = 1e-08
RATE_INPUT = 0.05
RATE_OUTPUT = 0.25
RATE_UP = 0.05
RATE_DOWN = 0.03
RATE_VECTOR = 0.1
RATE_OUTER = 0.3
WEIGHT_DECAY = 0.01


def layer_norm(features, norm_gain, norm_shift):
    row_mean = jnp.mean(features, axis=-1, keepdims=True)
    centered = features - row_mean
    spread = jnp.mean(centered * centered, axis=-1, keepdims=True)
    return centered * lax.rsqrt(spread + NORM_EPS) * norm_gain + norm_shift


def adam_update(weight, first_moment, second, gradient, step_rate, weight_decay):
    new_first = BETA * first_moment + (1.0 - BETA) * gradient
    new_second = BETA * second + (1.0 - BETA) * gradient * gradient
    correction = 1.0 - BETA**STEP
    step_ratio = new_first / correction / (jnp.sqrt(new_second / correction) + ADAM_EPS)
    return (weight - step_rate * (step_ratio + weight_decay * weight), new_first, new_second)


def row_scores(query_rows, key_rows, row_segments, score_scale):
    scores = (
        jnp.einsum("qhd,khd->hqk", query_rows, key_rows, preferred_element_type=jnp.float32)
        * score_scale
    )
    same_segment = row_segments[:, None] == row_segments[None, :]
    return jnp.where(same_segment[None], scores, NEG_FILL)


def attend_forward(query_heads, key_heads, value_heads, segment_ids, score_scale):

    def one_row(row_items):
        query_rows, key_rows, value_rows, row_segments = row_items
        scores = row_scores(query_rows, key_rows, row_segments, score_scale)
        row_peak = jnp.max(scores, axis=-1, keepdims=True)
        expo_terms = jnp.exp(scores - row_peak)
        row_total = jnp.sum(expo_terms, axis=-1, keepdims=True)
        soft_weights = (expo_terms / row_total).astype(jnp.bfloat16)
        attended = jnp.einsum(
            "hqk,khd->qhd", soft_weights, value_rows, preferred_element_type=jnp.float32
        )
        return (attended.astype(jnp.bfloat16), row_peak + jnp.log(row_total))

    return lax.map(one_row, (query_heads, key_heads, value_heads, segment_ids))


def attend_backward(
    query_heads, key_heads, value_heads, segment_ids, log_sums, grad_heads, score_scale
):

    def one_row(row_items):
        query_rows, key_rows, value_rows, row_segments, row_logsum, grad_rows = row_items
        scores = row_scores(query_rows, key_rows, row_segments, score_scale)
        back_weights = jnp.exp(scores - row_logsum)
        grad_soft = jnp.einsum(
            "qhd,khd->hqk", grad_rows, value_rows, preferred_element_type=jnp.float32
        )
        inner_terms = jnp.sum(back_weights * grad_soft, axis=-1, keepdims=True)
        grad_scores = (back_weights * (grad_soft - inner_terms)).astype(jnp.bfloat16)
        grad_query = (
            jnp.einsum("hqk,khd->qhd", grad_scores, key_rows, preferred_element_type=jnp.float32)
            * score_scale
        )
        grad_keys = (
            jnp.einsum("hqk,qhd->khd", grad_scores, query_rows, preferred_element_type=jnp.float32)
            * score_scale
        )
        grad_values = jnp.einsum(
            "hqk,qhd->khd",
            back_weights.astype(jnp.bfloat16),
            grad_rows,
            preferred_element_type=jnp.float32,
        )
        return (
            grad_query.astype(jnp.bfloat16),
            grad_keys.astype(jnp.bfloat16),
            grad_values.astype(jnp.bfloat16),
        )

    return lax.map(
        one_row, (query_heads, key_heads, value_heads, segment_ids, log_sums, grad_heads)
    )


def on_device(
    tokens,
    cotangent,
    segment_ids,
    input_weight,
    input_first,
    input_second,
    output_weight,
    output_first,
    output_second,
    up_weight,
    up_first,
    up_second,
    down_weight,
    down_first,
    down_second,
    inner_bias,
    inner_first,
    inner_second,
    vectors,
    vector_first,
    vector_second,
):
    input_full, output_full, up_full, down_full = (
        lax.all_gather(input_weight.astype(jnp.bfloat16), "dp", axis=1, tiled=True),
        lax.all_gather(output_weight.astype(jnp.bfloat16), "dp", axis=1, tiled=True),
        lax.all_gather(up_weight.astype(jnp.bfloat16), "dp", axis=0, tiled=True),
        lax.all_gather(down_weight.astype(jnp.bfloat16), "dp", axis=1, tiled=True),
    )
    tensor_count = lax.axis_size("tensor")
    tensor_index = lax.axis_index("tensor")
    token_count = tokens.shape[0]
    shard_rows = token_count // tensor_count
    row_count = segment_ids.shape[0]
    slot_count = segment_ids.shape[1]
    local_width = input_full.shape[2]
    head_local = local_width // DH
    score_scale = 1.0 / math.sqrt(DH)
    up_bias = inner_bias[2:].T.reshape(-1)

    def heads_view(flat_rows):
        return flat_rows.reshape(row_count, slot_count, head_local, DH)

    query_flat = (
        jnp.dot(tokens, input_full[0], preferred_element_type=jnp.float32) + inner_bias[0]
    ).astype(jnp.bfloat16)
    key_flat = jnp.dot(tokens, input_full[1], preferred_element_type=jnp.float32).astype(
        jnp.bfloat16
    )
    value_flat = (
        jnp.dot(tokens, input_full[2], preferred_element_type=jnp.float32) + inner_bias[1]
    ).astype(jnp.bfloat16)
    attended, log_sums = attend_forward(
        heads_view(query_flat),
        heads_view(key_flat),
        heads_view(value_flat),
        segment_ids,
        score_scale,
    )
    attended_flat = attended.reshape(token_count, local_width)
    attention_shard = lax.psum_scatter(
        jnp.dot(attended_flat, output_full, preferred_element_type=jnp.float32).astype(
            jnp.bfloat16
        ),
        "tensor",
        scatter_dimension=0,
        tiled=True,
    ).astype(jnp.float32)
    own_tokens = lax.dynamic_slice_in_dim(tokens, tensor_index * shard_rows, shard_rows, 0).astype(
        jnp.float32
    )
    pre_norm = own_tokens + (attention_shard + vectors[0])
    normed = layer_norm(pre_norm, vectors[1], vectors[2])
    normed_all = lax.all_gather(normed.astype(jnp.bfloat16), "tensor", axis=0, tiled=True)
    hidden_pre = jnp.dot(normed_all, up_full, preferred_element_type=jnp.float32) + up_bias
    hidden = jax.nn.gelu(hidden_pre, approximate=False).astype(jnp.bfloat16)
    feed_shard = lax.psum_scatter(
        jnp.dot(hidden, down_full, preferred_element_type=jnp.float32).astype(jnp.bfloat16),
        "tensor",
        scatter_dimension=0,
        tiled=True,
    ).astype(jnp.float32)
    pre_out = normed + (feed_shard + vectors[3])
    out_rows, out_pull = jax.vjp(layer_norm, pre_out, vectors[4], vectors[5])
    block_out = out_rows.astype(jnp.bfloat16)
    grad_pre_out, grad_gain_out, grad_shift_out = out_pull(cotangent.astype(jnp.float32))
    grad_feed_all = lax.all_gather(grad_pre_out.astype(jnp.bfloat16), "tensor", axis=0, tiled=True)
    down_grad = jnp.dot(hidden.T, grad_feed_all, preferred_element_type=jnp.float32)
    grad_hidden = jnp.dot(grad_feed_all, down_full.T, preferred_element_type=jnp.float32)
    gelu_pull = jax.vjp(partial(jax.nn.gelu, approximate=False), hidden_pre)[1]
    grad_hidden_pre = gelu_pull(grad_hidden)[0].astype(jnp.bfloat16)
    up_bias_grad = jnp.sum(grad_hidden_pre, axis=0, dtype=jnp.float32)
    up_grad = jnp.dot(normed_all.T, grad_hidden_pre, preferred_element_type=jnp.float32)
    normed_grad = grad_pre_out + lax.psum_scatter(
        jnp.dot(grad_hidden_pre, up_full.T, preferred_element_type=jnp.float32).astype(
            jnp.bfloat16
        ),
        "tensor",
        scatter_dimension=0,
        tiled=True,
    ).astype(jnp.float32)
    norm_pull = jax.vjp(layer_norm, pre_norm, vectors[1], vectors[2])[1]
    grad_pre_norm, grad_gain_in, grad_shift_in = norm_pull(normed_grad)
    grad_attention = lax.all_gather(
        grad_pre_norm.astype(jnp.bfloat16), "tensor", axis=0, tiled=True
    )
    output_grad = jnp.dot(attended_flat.T, grad_attention, preferred_element_type=jnp.float32)
    grad_attended = jnp.dot(
        grad_attention, output_full.T, preferred_element_type=jnp.float32
    ).astype(jnp.bfloat16)
    grad_query, grad_keys, grad_values = attend_backward(
        heads_view(query_flat),
        heads_view(key_flat),
        heads_view(value_flat),
        segment_ids,
        log_sums,
        heads_view(grad_attended),
        score_scale,
    )
    grad_query = grad_query.reshape(token_count, local_width)
    grad_keys = grad_keys.reshape(token_count, local_width)
    grad_values = grad_values.reshape(token_count, local_width)
    input_grad = jnp.stack(
        [
            jnp.dot(tokens.T, grad_query, preferred_element_type=jnp.float32),
            jnp.dot(tokens.T, grad_keys, preferred_element_type=jnp.float32),
            jnp.dot(tokens.T, grad_values, preferred_element_type=jnp.float32),
        ]
    )
    total = jnp.dot(grad_query, input_full[0].T, preferred_element_type=jnp.float32)
    total = total + jnp.dot(grad_keys, input_full[1].T, preferred_element_type=jnp.float32)
    token_grad = grad_pre_norm + lax.psum_scatter(
        (total + jnp.dot(grad_values, input_full[2].T, preferred_element_type=jnp.float32)).astype(
            jnp.bfloat16
        ),
        "tensor",
        scatter_dimension=0,
        tiled=True,
    ).astype(jnp.float32)
    inner_local = jnp.concatenate(
        [
            jnp.sum(grad_query, axis=0, dtype=jnp.float32)[None],
            jnp.sum(grad_values, axis=0, dtype=jnp.float32)[None],
            up_bias_grad.reshape(local_width, 4).T,
        ],
        axis=0,
    )
    inner_placed = lax.dynamic_update_slice(
        jnp.zeros((6, local_width * tensor_count), jnp.float32),
        inner_local,
        (0, tensor_index * local_width),
    )
    vector_local = jnp.stack(
        [
            jnp.sum(grad_pre_norm, axis=0),
            grad_gain_in,
            grad_shift_in,
            jnp.sum(grad_pre_out, axis=0),
            grad_gain_out,
            grad_shift_out,
        ]
    )
    inner_sum, vector_sum = lax.psum((inner_placed, vector_local), ("dp", "tensor"))
    inner_grad = lax.dynamic_slice_in_dim(inner_sum, tensor_index * local_width, local_width, 1)
    input_shard, output_shard, up_shard, down_shard = (
        lax.psum_scatter(input_grad, "dp", scatter_dimension=1, tiled=True),
        lax.psum_scatter(output_grad, "dp", scatter_dimension=1, tiled=True),
        lax.psum_scatter(up_grad, "dp", scatter_dimension=0, tiled=True),
        lax.psum_scatter(down_grad, "dp", scatter_dimension=1, tiled=True),
    )
    new_input = adam_update(
        input_weight, input_first, input_second, input_shard, RATE_INPUT, WEIGHT_DECAY
    )
    new_output = adam_update(
        output_weight, output_first, output_second, output_shard, RATE_OUTPUT, WEIGHT_DECAY
    )
    new_up = adam_update(up_weight, up_first, up_second, up_shard, RATE_UP, WEIGHT_DECAY)
    new_down = adam_update(
        down_weight, down_first, down_second, down_shard, RATE_DOWN, WEIGHT_DECAY
    )
    new_inner = adam_update(inner_bias, inner_first, inner_second, inner_grad, RATE_VECTOR, 0.0)
    new_vector = adam_update(vectors, vector_first, vector_second, vector_sum, RATE_OUTER, 0.0)
    return (
        block_out,
        token_grad,
        new_input[0],
        new_input[1],
        new_input[2],
        new_output[0],
        new_output[1],
        new_output[2],
        new_up[0],
        new_up[1],
        new_up[2],
        new_down[0],
        new_down[1],
        new_down[2],
        new_inner[0],
        new_inner[1],
        new_inner[2],
        new_vector[0],
        new_vector[1],
        new_vector[2],
    )


def solution(mesh):
    return jax.shard_map(
        on_device,
        mesh=mesh,
        in_specs=(
            P("dp", None),
            P(("dp", "tensor"), None),
            P("dp", None),
            P(None, "dp", "tensor"),
            P(None, "dp", "tensor"),
            P(None, "dp", "tensor"),
            P("tensor", "dp"),
            P("tensor", "dp"),
            P("tensor", "dp"),
            P("dp", "tensor"),
            P("dp", "tensor"),
            P("dp", "tensor"),
            P("tensor", "dp"),
            P("tensor", "dp"),
            P("tensor", "dp"),
            P(None, "tensor"),
            P(None, "tensor"),
            P(None, "tensor"),
            P(),
            P(),
            P(),
        ),
        out_specs=(
            P(("dp", "tensor"), None),
            P(("dp", "tensor"), None),
            P(None, "dp", "tensor"),
            P(None, "dp", "tensor"),
            P(None, "dp", "tensor"),
            P("tensor", "dp"),
            P("tensor", "dp"),
            P("tensor", "dp"),
            P("dp", "tensor"),
            P("dp", "tensor"),
            P("dp", "tensor"),
            P("tensor", "dp"),
            P("tensor", "dp"),
            P("tensor", "dp"),
            P(None, "tensor"),
            P(None, "tensor"),
            P(None, "tensor"),
            P(),
            P(),
            P(),
        ),
        check_vma=False,
    )
```

profile of v0, /device:TPU:0, one launch (start us, length us, event | category | flops | bytes accessed | tf_op | source)
XLA Modules:
  0.0 777.6 jit_solution(8586665917338929283)
XLA Ops:
  9.2 13.0 %all_gather.21 = bf16[3,768,192]{2,1,0:T(8,128)(2,1)S(1)} all-gather(bf16[3,96,192]{2,1,0:T(8,128)(2,1)S(1)} %convert_element_type.117), channel_id=1, replica_groups=mesh['dp'=8,'tensor'=4] {'dp'}, dimensions={1}, use_global_device_ids=true | all-gather | bytes 995328 | tf_op jit(solution)/shard_map/all_gather | solution.py:129
  23.0 4.0 convolution_convert_fusion.4
  48.6 26.9 %while.26 = (s32[]{:T(128)}, bf16[4,512,3,64]{1,3,2,0:T(8,128)(2,1)}, f32[4,3,512,1]{2,1,3,0:T(4,128)}, bf16[4,512,3,64]{1,3,2,0:T(8,128)(2,1)}, s32[4,512]{1,0:...) while((s32[]{:T(128)}, bf16[4,512,3,64]{1,3,2,0:T(8,128)(2,1)}, ...), condition=%wide.region_3.4_spmd, body=%wide.region_0.3_spmd.sunk | while | flops 211122688 | bytes 11332185 | solution.py:64
  79.1 9.4 %all_gather.22 = bf16[192,768]{0,1:T(8,128)(2,1)S(1)} all-gather(bf16[192,96]{0,1:T(8,128)(2,1)} %copy.117), channel_id=1, replica_groups=mesh['dp'=8,'tensor'=4] {'dp'}, dimensions={1}, use_global_device_ids=true | all-gather | bytes 331776 | tf_op jit(solution)/shard_map/all_gather | solution.py:130
  88.5 3.8 convolution_convert_fusion.2
  95.8 57.3 %reduce-scatter.13.cloned.1.call-done = bf16[512,768]{1,0:T(8,128)(2,1)} async-done(((bf16[2048,768]{1,0:T(8,128)(2,1)}), bf16[512,768]{1,0:T(8,128)(2,1)}) %reduce-scatter.13.cloned.1.call-update) | async-done | bytes 786448 | tf_op jit(solution)/shard_map/reduce_scatter | solution.py:165
  164.3 57.4 %all-gather.6.cloned.1.call-done = bf16[2048,768]{1,0:T(8,128)(2,1)} async-done(((bf16[512,768]{1,0:T(8,128)(2,1)}), bf16[2048,768]{1,0:T(8,128)(2,1)}) %all-gather.6.cloned.1.call-update) | async-done | bytes 3145744 | tf_op jit(solution)/shard_map/all_gather | solution.py:178
  221.7 18.9 %multiply_convert_fusion.1 = (bf16[2048,768]{1,0:T(8,128)(2,1)}, f32[2048,768]{1,0:T(8,128)}, f32[2048,768]{1,0:T(8,128)}) fusion(f32[768]{0:T(1024)} %add.262, bf16[2048,768]{1,0:T(8,128)(2,1)} %all-gather.6.cloned.1.call-done, bf16[768,768]{1,0:T(8,128)(2,1)} %all-gather.8.cloned.1.call-done), kind=kOutput, calls=%fused_computation.67 | convolution fusion | flops 2519728128 | bytes 20057088 | tf_op jit(solution)/shard_map/dot_general | solution.py:179
  240.6 6.0 all-gather.10.cloned.1.call-done
  246.6 6.5 convolution_convert_fusion.1
  253.6 60.0 %reduce-scatter.15.cloned.1.call-done = bf16[512,768]{1,0:T(8,128)(2,1)} async-done(((bf16[2048,768]{1,0:T(8,128)(2,1)}), bf16[512,768]{1,0:T(8,128)(2,1)}) %reduce-scatter.15.cloned.1.call-update) | async-done | bytes 786448 | tf_op jit(solution)/shard_map/reduce_scatter | solution.py:181
  322.0 63.4 %all-gather.12.cloned.1.call-done = bf16[2048,768]{1,0:T(8,128)(2,1)} async-done(((bf16[512,768]{1,0:T(8,128)(2,1)}), bf16[2048,768]{1,0:T(8,128)(2,1)}) %all-gather.12.cloned.1.call-update) | async-done | bytes 3145744 | tf_op jit(solution)/shard_map/all_gather | solution.py:191
  385.4 11.1 %convert_reduce_fusion = (f32[768]{0:T(1024)}, bf16[2048,768]{1,0:T(8,128)(2,1)S(1)}) fusion(f32[2048,768]{1,0:T(8,128)} %get-tuple-element.341, f32[2048,768]{1,0:T(8,128)} %get-tuple-element.351, f32[768]{0:T(1024)} %add.262, bf16[2048,768]{1,0:T(8,128)(2,1)} %all-gather.12.cloned.1.call-done, bf16[768,768]{0,1:T(8,128)(2,1)} %all-gather.10.cloned.1.call-done), kind=kOutput, calls=%fused_computation.64 | convolution fusion | flops 2442657024 | bytes 20060160 | tf_op jit(solution)/shard_map/dot_general | solution.py:193
  398.2 4.0 convolution_convert_fusion
  402.3 59.0 %reduce-scatter.17.cloned.1.call-done = bf16[512,768]{1,0:T(8,128)(2,1)} async-done(((bf16[2048,768]{1,0:T(8,128)(2,1)}), bf16[512,768]{1,0:T(8,128)(2,1)}) %reduce-scatter.17.cloned.1.call-update) | async-done | bytes 786448 | tf_op jit(solution)/shard_map/reduce_scatter | solution.py:198
  469.9 7.0 fusion.92
  476.9 7.4 fusion.91
  484.4 48.7 %all-gather.14.cloned.1.call-done = bf16[2048,768]{1,0:T(8,128)(2,1)} async-done(((bf16[512,768]{1,0:T(8,128)(2,1)}), bf16[2048,768]{1,0:T(8,128)(2,1)}) %all-gather.14.cloned.1.call-update) | async-done | bytes 3145744 | tf_op jit(solution)/shard_map/all_gather | solution.py:208
  533.2 4.0 convolution_convert_fusion.3
  545.3 40.0 %while.27 = (s32[]{:T(128)}, bf16[4,512,3,64]{1,3,2,0:T(8,128)(2,1)}, bf16[4,512,3,64]{1,3,2,0:T(8,128)(2,1)}, bf16[4,512,3,64]{1,3,2,0:T(8,128)(2,1)}, bf16[4,5...) while((s32[]{:T(128)}, ...), condition=%wide.region_17.18_spmd, body=%wide.region_15.17_spmd.sunk | while | flops 511146496 | bytes 32418988 | solution.py:100
  615.1 8.4 %reduce-scatter.21.cloned.1.call-done = f32[96,768]{1,0:T(8,128)} async-done(((f32[768,768]{1,0:T(8,128)}), f32[96,768]{1,0:T(8,128)}) %reduce-scatter.21.cloned.1.call-update) | async-done | bytes 294928 | tf_op jit(solution)/shard_map/reduce_scatter | solution.py:272
  627.7 39.9 %all-reduce = (f32[6,768]{1,0:T(8,128)S(1)}, f32[6,768]{1,0:T(8,128)S(1)}) all-reduce(f32[6,768]{1,0:T(8,128)S(1)} %dynamic_update_slice.20, f32[6,768]{1,0:T(8,128)S(1)} %stack.31), channel_id=1, replica_groups=mesh['dp'=8,'tensor'=4] {'dp','tensor'}, use_global_device_ids=true, to_apply=%region_26.27 | all-reduce | flops 9216 | bytes 73728 | tf_op jit(solution)/shard_map/psum | solution.py:267
  670.8 34.1 %reduce-scatter.25.cloned.1.call-done = f32[96,576]{1,0:T(8,128)} async-done(((f32[768,576]{1,0:T(8,128)}), f32[96,576]{1,0:T(8,128)}) %reduce-scatter.25.cloned.1.call-update) | async-done | bytes 221200
  710.8 56.9 %reduce-scatter.19.cloned.1.call-done = bf16[512,768]{1,0:T(8,128)(2,1)} async-done(((bf16[2048,768]{1,0:T(8,128)(2,1)}), bf16[512,768]{1,0:T(8,128)(2,1)}) %reduce-scatter.19.cloned.1.call-update) | async-done | bytes 786448 | tf_op jit(solution)/shard_map/reduce_scatter | solution.py:236
  (293 shorter events, 180.7 us)
Async XLA Ops:
  8.0 19.0 %copy-start = (bf16[2048,768]{1,0:T(8,128)(2,1)S(1)}, bf16[2048,768]{1,0:T(8,128)(2,1)}, u32[]{:S(2)}) copy-start(bf16[2048,768]{1,0:T(8,128)(2,1)} %param.25) | copy-start | bytes 9437188
  8.0 145.1 %reduce-scatter.13.cloned.1.call-start = ((), (), s32[]{:S(2)}) async-start(), calls=%async_computation.8 | async-start | bytes 3932160 | tf_op jit(solution)/shard_map/reduce_scatter | solution.py:165
  92.4 71.9 %all-gather.8.cloned.1.call-start = ((), (), s32[]{:S(2)}) async-start(), calls=%async_computation.10 | async-start | bytes 1327104 | tf_op jit(solution)/shard_map/all_gather | solution.py:131
  94.1 127.5 %all-gather.6.cloned.1.call-start = ((), (), s32[]{:S(2)}) async-start(), calls=%async_computation.9 | async-start | bytes 3932160 | tf_op jit(solution)/shard_map/all_gather | solution.py:178
  158.2 88.4 %all-gather.10.cloned.1.call-start = ((), (), s32[]{:S(2)}) async-start(), calls=%async_computation.11 | async-start | bytes 1327104 | tf_op jit(solution)/shard_map/all_gather | solution.py:132
  159.9 153.6 %reduce-scatter.15.cloned.1.call-start = ((), (), s32[]{:S(2)}) async-start(), calls=%async_computation.12 | async-start | bytes 3932160 | tf_op jit(solution)/shard_map/reduce_scatter | solution.py:181
  253.1 132.3 %all-gather.12.cloned.1.call-start = ((), (), s32[]{:S(2)}) async-start(), calls=%async_computation.13 | async-start | bytes 3932160 | tf_op jit(solution)/shard_map/all_gather | solution.py:191
  322.0 139.3 %reduce-scatter.17.cloned.1.call-start = ((), (), s32[]{:S(2)}) async-start(), calls=%async_computation.14 | async-start | bytes 3932160 | tf_op jit(solution)/shard_map/reduce_scatter | solution.py:198
  402.2 130.9 %all-gather.14.cloned.1.call-start = ((), (), s32[]{:S(2)}) async-start(), calls=%async_computation.15 | async-start | bytes 3932160 | tf_op jit(solution)/shard_map/all_gather | solution.py:208
  469.7 143.2 %reduce-scatter.23.cloned.1.call-start = ((), (), s32[]{:S(2)}) async-start(), calls=%async_computation.18 | async-start | bytes 2654208 | tf_op jit(solution)/shard_map/reduce_scatter | solution.py:273
  476.9 146.6 %reduce-scatter.21.cloned.1.call-start = ((), (), s32[]{:S(2)}) async-start(), calls=%async_computation.17 | async-start | bytes 2654208 | tf_op jit(solution)/shard_map/reduce_scatter | solution.py:272
  484.4 184.7 %reduce-scatter.27.cloned.1.call-start = ((), (), s32[]{:S(2)}) async-start(), calls=%async_computation.20 | async-start | bytes 884736
  591.8 113.1 %reduce-scatter.25.cloned.1.call-start = ((), (), s32[]{:S(2)}) async-start(), calls=%async_computation.19 | async-start | bytes 2211840
  604.7 163.0 %reduce-scatter.19.cloned.1.call-start = ((), (), s32[]{:S(2)}) async-start(), calls=%async_computation.16 | async-start | bytes 3932160 | tf_op jit(solution)/shard_map/reduce_scatter | solution.py:236
  612.5 55.1 %copy-start.35 = (f32[6,192]{1,0:T(8,128)S(1)}, f32[6,192]{1,0:T(8,128)}, u32[]{:S(2)}) copy-start(f32[6,192]{1,0:T(8,128)} %param.40) | copy-start | bytes 13828
  612.5 55.1 %copy-start.45 = (f32[6,192]{1,0:T(8,128)S(1)}, f32[6,192]{1,0:T(8,128)}, u32[]{:S(2)}) copy-start(f32[6,192]{1,0:T(8,128)} %param.41) | copy-start | bytes 13828
  612.6 55.1 %copy-start.46 = (f32[6,192]{1,0:T(8,128)S(1)}, f32[6,192]{1,0:T(8,128)}, u32[]{:S(2)}) copy-start(f32[6,192]{1,0:T(8,128)} %param.42) | copy-start | bytes 13828
  612.6 55.8 %copy-start.31 = (f32[6,768]{1,0:T(8,128)S(1)}, f32[6,768]{1,0:T(8,128)}, u32[]{:S(2)}) copy-start(f32[6,768]{1,0:T(8,128)} %param.43) | copy-start | bytes 55300
  612.6 55.8 %copy-start.36 = (f32[6,768]{1,0:T(8,128)S(1)}, f32[6,768]{1,0:T(8,128)}, u32[]{:S(2)}) copy-start(f32[6,768]{1,0:T(8,128)} %param.44) | copy-start | bytes 55300
  612.6 55.8 %copy-start.37 = (f32[6,768]{1,0:T(8,128)S(1)}, f32[6,768]{1,0:T(8,128)}, u32[]{:S(2)}) copy-start(f32[6,768]{1,0:T(8,128)} %param.45) | copy-start | bytes 55300
  612.9 57.2 %copy-start.25 = (f32[192,96]{1,0:T(8,128)S(1)}, f32[192,96]{1,0:T(8,128)}, u32[]{:S(2)}) copy-start(f32[192,96]{1,0:T(8,128)} %param.31) | copy-start | bytes 221188
  612.9 57.2 %copy-start.29 = (f32[192,96]{1,0:T(8,128)S(1)}, f32[192,96]{1,0:T(8,128)}, u32[]{:S(2)}) copy-start(f32[192,96]{1,0:T(8,128)} %param.32) | copy-start | bytes 221188
  612.9 57.2 %copy-start.30 = (f32[192,96]{1,0:T(8,128)S(1)}, f32[192,96]{1,0:T(8,128)}, u32[]{:S(2)}) copy-start(f32[192,96]{1,0:T(8,128)} %param.33) | copy-start | bytes 221188
  667.7 100.0 %copy-start.8 = (f32[512,768]{1,0:T(8,128)S(1)}, f32[512,768]{1,0:T(8,128)}, u32[]{:S(2)}) copy-start(f32[512,768]{1,0:T(8,128)} %copy-done.7) | copy-start | bytes 4718596
  (45 other events, 180.9 us)
Sparse Core Ops, SparseCore 0:
  92.5 60.5 reduce-scatter.12
  253.2 60.2 reduce-scatter.14
  402.4 58.8 reduce-scatter.16
Sparse Core Ops, SparseCore 1:
  95.3 24.1 all-gather.7
  158.3 63.3 all-gather.5
  224.0 22.5 all-gather.9
  322.0 63.3 all-gather.11
  469.7 63.3 all-gather.13
  536.5 41.0 reduce-scatter.22
  581.1 42.3 reduce-scatter.20
  626.5 34.9 reduce-scatter.26
  664.7 40.1 reduce-scatter.24
  707.4 60.2 reduce-scatter.18
where the time goes:
time: 788 us; the launch traced here: 778 us
  waiting for transfers between devices  451 us (57%)
  matrix products  133 us (17%)
  local copies, waits for them, and re-layouts  66.3 us (8%)
  blocking collectives  62.4 us (8%)
  other arithmetic  46.4 us (6%)
  between operations  16.4 us (2%)
    all_gather x1, waiting for transfers between devices, on_device(): lax.all_gather(grad_pre_out.astype(jnp.bfloat16), 'tensor', axis=0, tiled...  63.4 us
    reduce_scatter x1, waiting for transfers between devices, on_device(): lax.psum_scatter(jnp.dot(hidden, down_full, preferred_element_type=jnp.fl...  60 us
    reduce_scatter x1, waiting for transfers between devices, on_device(): lax.psum_scatter(jnp.dot(grad_hidden_pre, up_full.T, preferred_element_ty...  59 us
    all_gather x1, waiting for transfers between devices, on_device(): lax.all_gather(normed.astype(jnp.bfloat16), 'tensor', axis=0, tiled=True)  57.4 us
    reduce_scatter x1, waiting for transfers between devices, on_device(): lax.psum_scatter(jnp.dot(attended_flat, output_full, preferred_element_ty...  57.3 us
    reduce_scatter x1, waiting for transfers between devices, on_device(): lax.psum_scatter((total + jnp.dot(grad_values, input_full[2].T, preferred...  56.9 us
    all_gather x1, waiting for transfers between devices, on_device(): lax.all_gather(grad_pre_norm.astype(jnp.bfloat16), 'tensor', axis=0, tile...  48.7 us
    psum x1, blocking collectives, on_device(): lax.psum((inner_placed, vector_local), ('dp', 'tensor'))  39.9 us
  transfers between devices with their start and end apart: 13, of which 10 were waited for; matrix products, arithmetic and copies ran while one was open for 18% of the time, Pallas kernels for 0%

commit v1 on v0

--- a/solution.py
+++ b/solution.py
@@ -125,34 +125,49 @@
     vector_first,
     vector_second,
 ):
-    input_full, output_full, up_full, down_full = (
-        lax.all_gather(input_weight.astype(jnp.bfloat16), "dp", axis=1, tiled=True),
-        lax.all_gather(output_weight.astype(jnp.bfloat16), "dp", axis=1, tiled=True),
-        lax.all_gather(up_weight.astype(jnp.bfloat16), "dp", axis=0, tiled=True),
-        lax.all_gather(down_weight.astype(jnp.bfloat16), "dp", axis=1, tiled=True),
-    )
+    axes = ("dp", "tensor")
+
+    def gather_whole(shard, dp_dim, tensor_dim):
+        low_shard = shard.astype(jnp.bfloat16)
+        part = lax.all_gather(low_shard, "dp", axis=dp_dim, tiled=True)
+        return lax.all_gather(part, "tensor", axis=tensor_dim, tiled=True)
+
+    def scatter_sum(whole, dp_dim, tensor_dim):
+        part = lax.psum_scatter(
+            whole.astype(jnp.bfloat16), "tensor", scatter_dimension=tensor_dim, tiled=True
+        )
+        return lax.psum_scatter(part, "dp", scatter_dimension=dp_dim, tiled=True).astype(
+            jnp.float32
+        )
+
+    input_full = gather_whole(input_weight, 1, 2)
+    output_full = gather_whole(output_weight, 1, 0)
+    up_full = gather_whole(up_weight, 0, 1)
+    down_full = gather_whole(down_weight, 1, 0)
+    bias_full = lax.all_gather(inner_bias, "tensor", axis=1, tiled=True)
     tensor_count = lax.axis_size("tensor")
     tensor_index = lax.axis_index("tensor")
-    token_count = tokens.shape[0]
-    shard_rows = token_count // tensor_count
-    row_count = segment_ids.shape[0]
+    row_count = segment_ids.shape[0] // tensor_count
     slot_count = segment_ids.shape[1]
-    local_width = input_full.shape[2]
-    head_local = local_width // DH
+    token_count = row_count * slot_count
+    width = tokens.shape[1]
+    head_count = width // DH
     score_scale = 1.0 / math.sqrt(DH)
-    up_bias = inner_bias[2:].T.reshape(-1)
+    tokens = lax.dynamic_slice_in_dim(tokens, tensor_index * token_count, token_count, 0)
+    segment_ids = lax.dynamic_slice_in_dim(segment_ids, tensor_index * row_count, row_count, 0)
+    up_bias = bias_full[2:].T.reshape(-1)
 
     def heads_view(flat_rows):
-        return flat_rows.reshape(row_count, slot_count, head_local, DH)
+        return flat_rows.reshape(row_count, slot_count, head_count, DH)
 
     query_flat = (
-        jnp.dot(tokens, input_full[0], preferred_element_type=jnp.float32) + inner_bias[0]
+        jnp.dot(tokens, input_full[0], preferred_element_type=jnp.float32) + bias_full[0]
     ).astype(jnp.bfloat16)
     key_flat = jnp.dot(tokens, input_full[1], preferred_element_type=jnp.float32).astype(
         jnp.bfloat16
     )
     value_flat = (
-        jnp.dot(tokens, input_full[2], preferred_element_type=jnp.float32) + inner_bias[1]
+        jnp.dot(tokens, input_full[2], preferred_element_type=jnp.float32) + bias_full[1]
     ).astype(jnp.bfloat16)
     attended, log_sums = attend_forward(
         heads_view(query_flat),
@@ -161,54 +176,40 @@
         segment_ids,
         score_scale,
     )
-    attended_flat = attended.reshape(token_count, local_width)
-    attention_shard = lax.psum_scatter(
-        jnp.dot(attended_flat, output_full, preferred_element_type=jnp.float32).astype(
-            jnp.bfloat16
-        ),
-        "tensor",
-        scatter_dimension=0,
-        tiled=True,
-    ).astype(jnp.float32)
-    own_tokens = lax.dynamic_slice_in_dim(tokens, tensor_index * shard_rows, shard_rows, 0).astype(
-        jnp.float32
-    )
-    pre_norm = own_tokens + (attention_shard + vectors[0])
+    attended_flat = attended.reshape(token_count, width)
+    pre_norm = tokens.astype(jnp.float32) + (
+        jnp.dot(attended_flat, output_full, preferred_element_type=jnp.float32) + vectors[0]
+    )
     normed = layer_norm(pre_norm, vectors[1], vectors[2])
-    normed_all = lax.all_gather(normed.astype(jnp.bfloat16), "tensor", axis=0, tiled=True)
-    hidden_pre = jnp.dot(normed_all, up_full, preferred_element_type=jnp.float32) + up_bias
+    normed_low = normed.astype(jnp.bfloat16)
+    hidden_pre = jnp.dot(normed_low, up_full, preferred_element_type=jnp.float32) + up_bias
     hidden = jax.nn.gelu(hidden_pre, approximate=False).astype(jnp.bfloat16)
-    feed_shard = lax.psum_scatter(
-        jnp.dot(hidden, down_full, preferred_element_type=jnp.float32).astype(jnp.bfloat16),
-        "tensor",
-        scatter_dimension=0,
-        tiled=True,
-    ).astype(jnp.float32)
-    pre_out = normed + (feed_shard + vectors[3])
+    pre_out = normed + (
+        jnp.dot(hidden, down_full, preferred_element_type=jnp.float32) + vectors[3]
+    )
     out_rows, out_pull = jax.vjp(layer_norm, pre_out, vectors[4], vectors[5])
     block_out = out_rows.astype(jnp.bfloat16)
     grad_pre_out, grad_gain_out, grad_shift_out = out_pull(cotangent.astype(jnp.float32))
-    grad_feed_all = lax.all_gather(grad_pre_out.astype(jnp.bfloat16), "tensor", axis=0, tiled=True)
-    down_grad = jnp.dot(hidden.T, grad_feed_all, preferred_element_type=jnp.float32)
-    grad_hidden = jnp.dot(grad_feed_all, down_full.T, preferred_element_type=jnp.float32)
+    grad_feed = grad_pre_out.astype(jnp.bfloat16)
+    down_shard = scatter_sum(
+        jnp.dot(hidden.T, grad_feed, preferred_element_type=jnp.float32), 1, 0
+    )
+    grad_hidden = jnp.dot(grad_feed, down_full.T, preferred_element_type=jnp.float32)
     gelu_pull = jax.vjp(partial(jax.nn.gelu, approximate=False), hidden_pre)[1]
     grad_hidden_pre = gelu_pull(grad_hidden)[0].astype(jnp.bfloat16)
     up_bias_grad = jnp.sum(grad_hidden_pre, axis=0, dtype=jnp.float32)
-    up_grad = jnp.dot(normed_all.T, grad_hidden_pre, preferred_element_type=jnp.float32)
-    normed_grad = grad_pre_out + lax.psum_scatter(
-        jnp.dot(grad_hidden_pre, up_full.T, preferred_element_type=jnp.float32).astype(
-            jnp.bfloat16
-        ),
-        "tensor",
-        scatter_dimension=0,
-        tiled=True,
-    ).astype(jnp.float32)
+    up_shard = scatter_sum(
+        jnp.dot(normed_low.T, grad_hidden_pre, preferred_element_type=jnp.float32), 0, 1
+    )
+    normed_grad = grad_pre_out + jnp.dot(
+        grad_hidden_pre, up_full.T, preferred_element_type=jnp.float32
+    )
     norm_pull = jax.vjp(layer_norm, pre_norm, vectors[1], vectors[2])[1]
     grad_pre_norm, grad_gain_in, grad_shift_in = norm_pull(normed_grad)
-    grad_attention = lax.all_gather(
-        grad_pre_norm.astype(jnp.bfloat16), "tensor", axis=0, tiled=True
-    )
-    output_grad = jnp.dot(attended_flat.T, grad_attention, preferred_element_type=jnp.float32)
+    grad_attention = grad_pre_norm.astype(jnp.bfloat16)
+    output_shard = scatter_sum(
+        jnp.dot(attended_flat.T, grad_attention, preferred_element_type=jnp.float32), 1, 0
+    )
     grad_attended = jnp.dot(
         grad_attention, output_full.T, preferred_element_type=jnp.float32
     ).astype(jnp.bfloat16)
@@ -221,38 +222,32 @@
         heads_view(grad_attended),
         score_scale,
     )
-    grad_query = grad_query.reshape(token_count, local_width)
-    grad_keys = grad_keys.reshape(token_count, local_width)
-    grad_values = grad_values.reshape(token_count, local_width)
-    input_grad = jnp.stack(
-        [
-            jnp.dot(tokens.T, grad_query, preferred_element_type=jnp.float32),
-            jnp.dot(tokens.T, grad_keys, preferred_element_type=jnp.float32),
-            jnp.dot(tokens.T, grad_values, preferred_element_type=jnp.float32),
-        ]
+    grad_query = grad_query.reshape(token_count, width)
+    grad_keys = grad_keys.reshape(token_count, width)
+    grad_values = grad_values.reshape(token_count, width)
+    input_shard = scatter_sum(
+        jnp.stack(
+            [
+                jnp.dot(tokens.T, grad_query, preferred_element_type=jnp.float32),
+                jnp.dot(tokens.T, grad_keys, preferred_element_type=jnp.float32),
+                jnp.dot(tokens.T, grad_values, preferred_element_type=jnp.float32),
+            ]
+        ),
+        1,
+        2,
     )
     total = jnp.dot(grad_query, input_full[0].T, preferred_element_type=jnp.float32)
     total = total + jnp.dot(grad_keys, input_full[1].T, preferred_element_type=jnp.float32)
-    token_grad = grad_pre_norm + lax.psum_scatter(
-        (total + jnp.dot(grad_values, input_full[2].T, preferred_element_type=jnp.float32)).astype(
-            jnp.bfloat16
-        ),
-        "tensor",
-        scatter_dimension=0,
-        tiled=True,
-    ).astype(jnp.float32)
+    token_grad = grad_pre_norm + (
+        total + jnp.dot(grad_values, input_full[2].T, preferred_element_type=jnp.float32)
+    )
     inner_local = jnp.concatenate(
         [
             jnp.sum(grad_query, axis=0, dtype=jnp.float32)[None],
             jnp.sum(grad_values, axis=0, dtype=jnp.float32)[None],
-            up_bias_grad.reshape(local_width, 4).T,
+            up_bias_grad.reshape(width, 4).T,
         ],
         axis=0,
-    )
-    inner_placed = lax.dynamic_update_slice(
-        jnp.zeros((6, local_width * tensor_count), jnp.float32),
-        inner_local,
-        (0, tensor_index * local_width),
     )
     vector_local = jnp.stack(
         [
@@ -264,14 +259,9 @@
             grad_shift_out,
         ]
     )
-    inner_sum, vector_sum = lax.psum((inner_placed, vector_local), ("dp", "tensor"))
+    inner_sum, vector_sum = lax.psum((inner_local, vector_local), axes)
+    local_width = width // tensor_count
     inner_grad = lax.dynamic_slice_in_dim(inner_sum, tensor_index * local_width, local_width, 1)
-    input_shard, output_shard, up_shard, down_shard = (
-        lax.psum_scatter(input_grad, "dp", scatter_dimension=1, tiled=True),
-        lax.psum_scatter(output_grad, "dp", scatter_dimension=1, tiled=True),
-        lax.psum_scatter(up_grad, "dp", scatter_dimension=0, tiled=True),
-        lax.psum_scatter(down_grad, "dp", scatter_dimension=1, tiled=True),
-    )
     new_input = adam_update(
         input_weight, input_first, input_second, input_shard, RATE_INPUT, WEIGHT_DECAY
     )

time: 788 us -> 842 us (1.069)
  waiting for transfers between devices: 451 us -> 558 us
  local copies, waits for them, and re-layouts: 66.3 us -> 36.4 us
  matrix products: 133 us -> 106 us
  blocking collectives: 62.4 us -> 86.7 us
  other arithmetic: 46.4 us -> 30.4 us
    unnamed x15 -> x17, waiting for transfers between devices: 34.3 us -> 116 us
    all_gather x5 -> x6, waiting for transfers between devices: 175 us -> 251 us  [the longest x4 240 us: gather_whole(): return lax.all_gather(part, 'tensor', axis=tensor_dim, tiled=True)]
    reduce_scatter x6 -> x5, waiting for transfers between devices: 242 us -> 190 us  [the longest x3 115 us: scatter_sum(): lax.psum_scatter(whole.astype(jnp.bfloat16), 'tensor', scatter_dimension=...]
    all_gather x2 -> x3, blocking collectives: 22.5 us -> 38.7 us  [the longest x2 25.6 us: gather_whole(): part = lax.all_gather(low_shard, 'dp', axis=dp_dim, tiled=True)]
    while x24 -> x0, local copies, waits for them, and re-layouts: 13.7 us -> none  [the longest x4 8.31 us: attend_forward(): return lax.map(one_row, (query_heads, key_heads, value_heads, segment_ids))]
    reshape x5 -> x1, local copies, waits for them, and re-layouts: 12 us -> 0.39 us  [on_device(): up_bias_grad.reshape(width, 4)]
    dot_general x8 -> x1, matrix products: 11.8 us -> 2.07 us  [row_scores(): jnp.einsum('qhd,khd->hqk', query_rows, key_rows, preferred_element_type=j...]
    unnamed x112 -> x117, local copies, waits for them, and re-layouts: 20.9 us -> 29 us
  transfers between devices with their start and end apart: 13 -> 14, of which waited for: 10 -> 12; matrix products, arithmetic and copies ran while one was open for 18% -> 16% of each run, Pallas kernels for 0% -> 0%
where the time goes in v1:
time: 842 us; the launch traced here: 833 us
  waiting for transfers between devices  558 us (66%)
  matrix products  106 us (13%)
  blocking collectives  86.7 us (10%)
  local copies, waits for them, and re-layouts  36.4 us (4%)
  other arithmetic  30.4 us (4%)
  between operations  15.2 us (2%)
    all_gather x4, waiting for transfers between devices, gather_whole(): return lax.all_gather(part, 'tensor', axis=tensor_dim, tiled=True)  240 us
    unnamed x17, waiting for transfers between devices  116 us
    reduce_scatter x3, waiting for transfers between devices, scatter_sum(): lax.psum_scatter(whole.astype(jnp.bfloat16), 'tensor', scatter_dimension=...  115 us
    reduce_scatter x2, waiting for transfers between devices, scatter_sum(): lax.psum_scatter(part, 'dp', scatter_dimension=dp_dim, tiled=True)  74.9 us
    psum x1, blocking collectives, on_device(): inner_sum, vector_sum = lax.psum((inner_local, vector_local), axes)  48 us
    unnamed x117, local copies, waits for them, and re-layouts  29 us
    all_gather x2, blocking collectives, gather_whole(): part = lax.all_gather(low_shard, 'dp', axis=dp_dim, tiled=True)  25.6 us
    dot_general x1, matrix products, on_device(): jnp.dot(normed_low, up_full, preferred_element_type=jnp.float32) + up_bias  19.6 us
  transfers between devices with their start and end apart: 14, of which 12 were waited for; matrix products, arithmetic and copies ran while one was open for 16% of the time, Pallas kernels for 0%

profile of v1, /device:TPU:0, one launch (start us, length us, event | category | flops | bytes accessed | tf_op | source)
XLA Modules:
  0.0 833.2 jit_solution(13847416268812495529)
XLA Ops:
  11.8 16.2 %all_gather.27 = bf16[3,768,192]{2,0,1:T(4,128)(2,1)S(1)} all-gather(bf16[3,96,192]{2,0,1:T(4,128)(2,1)S(1)} %copy.164), channel_id=1, replica_groups=mesh['dp'=8,'tensor'=4] {'dp'}, dimensions={1}, use_global_device_ids=true | all-gather | bytes 995328 | tf_op jit(solution)/shard_map/all_gather | solution.py:132
  30.2 9.3 %all_gather.30 = bf16[192,768]{0,1:T(8,128)(2,1)S(1)} all-gather(bf16[192,96]{0,1:T(8,128)(2,1)S(1)} %copy.171), channel_id=1, replica_groups=mesh['dp'=8,'tensor'=4] {'dp'}, dimensions={1}, use_global_device_ids=true | all-gather | bytes 331776 | tf_op jit(solution)/shard_map/all_gather | solution.py:132
  41.1 13.2 %all-gather = f32[4,192,6]{1,2,0:T(8,128)S(1)} all-gather(f32[1,192,6]{1,2,0:T(8,128)S(1)} %bitcast.111), channel_id=1, replica_groups=mesh['dp'=8,'tensor'=4] {'tensor'}, dimensions={0}, use_global_device_ids=true | all-gather | bytes 23040 | tf_op jit(solution)/shard_map/all_gather | solution.py:147
  55.1 11.2 %all-gather.16.cloned.1.call-done = bf16[768,768]{0,1:T(8,128)(2,1)} async-done(((bf16[768,96]{0,1:T(8,128)(2,1)}), bf16[768,768]{0,1:T(8,128)(2,1)}) %all-gather.16.cloned.1.call-update) | async-done | bytes 1179664 | tf_op jit(solution)/shard_map/all_gather | solution.py:132
  66.5 72.1 %all-gather.8.cloned.1.call-done = bf16[3,768,768]{1,2,0:T(8,128)(2,1)} async-done(((bf16[3,768,192]{1,2,0:T(8,128)(2,1)}), bf16[3,768,768]{1,2,0:T(8,128)(2,1)}) %all-gather.8.cloned.1.call-update) | async-done | bytes 3538960 | tf_op jit(solution)/shard_map/all_gather | solution.py:133
  158.1 11.5 %all-gather.10.cloned.1.call-done = bf16[768,768]{1,0:T(8,128)(2,1)} async-done(((bf16[192,768]{1,0:T(8,128)(2,1)}), bf16[768,768]{1,0:T(8,128)(2,1)}) %all-gather.10.cloned.1.call-update) | async-done | bytes 1179664 | tf_op jit(solution)/shard_map/all_gather | solution.py:133
  172.7 87.0 %all-gather.14.cloned.1.call-done = bf16[768,3072]{1,0:T(8,128)(2,1)} async-done(((bf16[768,768]{1,0:T(8,128)(2,1)}), bf16[768,3072]{1,0:T(8,128)(2,1)}) %all-gather.14.cloned.1.call-update) | async-done | bytes 4718608 | tf_op jit(solution)/shard_map/all_gather | solution.py:133
  259.6 19.6 %multiply_convert_fusion.1 = (bf16[512,3072]{1,0:T(8,128)(2,1)}, f32[512,3072]{1,0:T(8,128)}, f32[512,3072]{1,0:T(8,128)}) fusion(f32[3072]{0:T(1024)S(1)} %add.257, bf16[768,3072]{1,0:T(8,128)(2,1)} %all-gather.14.cloned.1.call-done, f32[512,768]{1,0:T(8,128)S(1)} %get-tuple-element.215, f32[768]{0:T(1024)S(1)} %get-tuple-element.179, ...), kind=kOutput, calls=%fused_computation.14 | convolution fusion | flops 2521694208 | bytes 22042624 | tf_op jit(solution)/shard_map/dot_general | solution.py:185
  279.3 69.6 %all-gather.18.cloned.1.call-done = bf16[3072,768]{0,1:T(8,128)(2,1)} async-done(((bf16[768,768]{0,1:T(8,128)(2,1)}), bf16[3072,768]{0,1:T(8,128)(2,1)}) %all-gather.18.cloned.1.call-update) | async-done | bytes 4718608 | tf_op jit(solution)/shard_map/all_gather | solution.py:133
  348.9 6.2 fusion.65
  358.4 8.4 %convert_reduce_fusion = (f32[3072]{0:T(1024)}, bf16[512,3072]{1,0:T(8,128)(2,1)S(1)}) fusion(f32[512,3072]{1,0:T(8,128)S(1)} %copy-done.48, bf16[3072,768]{0,1:T(8,128)(2,1)S(1)} %copy-done.44, f32[512,768]{1,0:T(8,128)S(1)} %get-tuple-element.208, f32[512]{0:T(512)S(1)} %negate_multiply_fusion.2, f32[512,3072]{1,0:T(8,128)} %get-tuple-element.216, ...), kind=kOutput, calls=%fused_computation.11 | convolution fusion | flops 2443441152 | bytes 22046720 | tf_op jit(solution)/shard_map/dot_general | solution.py:197
  380.0 13.8 %multiply_reduce_fusion = (f32[12,512]{1,0:T(8,128)S(1)}, f32[12,512,512]{1,2,0:T(8,128)}) fusion(f32[12,512]{1,0:T(8,128)S(1)} %log_add_fusion, f32[12,512,512]{1,2,0:T(8,128)} %copy-done.2, pred[512,512]{0,1:T(8,128)(4,1)S(1)} %broadcast_compare_fusion, bf16[512,12,64]{0,2,1:T(8,128)(2,1)} %bitcast.98, bf16[512,12,64]{0,2,1:T(8,128)(2,1)} %bitcast.97), kind=kOutput, calls=%fused_computation.1 | convolution fusion | flops 418375680 | bytes 27049984 | tf_op jit(solution)/shard_map/while/body/eval_jaxpr/qhd,khd->hqk/dot_general | solution.py:75
  393.8 7.6 multiply_convert_fusion
  414.5 5.7 copy.184
  426.5 6.8 convolution_convert_fusion
  434.7 6.7 convolution_convert_fusion.1
  443.5 46.3 %reduce-scatter.25.cloned.1.call-done = bf16[192,2304]{1,0:T(8,128)(2,1)} async-done(((bf16[768,2304]{1,0:T(8,128)(2,1)}), bf16[192,2304]{1,0:T(8,128)(2,1)}) %reduce-scatter.25.cloned.1.call-update) | async-done | bytes 884752
  496.6 81.2 %reduce-scatter.23.cloned.1.call-done = bf16[768,768]{1,0:T(8,128)(2,1)} async-done(((bf16[3072,768]{1,0:T(8,128)(2,1)}), bf16[768,768]{1,0:T(8,128)(2,1)}) %reduce-scatter.23.cloned.1.call-update) | async-done | bytes 1179664 | tf_op jit(solution)/shard_map/reduce_scatter | solution.py:136
  581.5 48.0 %all-reduce = (f32[6,768]{1,0:T(8,128)S(1)}, f32[6,768]{1,0:T(8,128)S(1)}) all-reduce(f32[6,768]{1,0:T(8,128)S(1)} %pad_maximum_fusion.1, f32[6,768]{1,0:T(8,128)S(1)} %stack.35), channel_id=1, replica_groups=mesh['dp'=8,'tensor'=4] {'dp','tensor'}, use_global_device_ids=true, to_apply=%region_22.23 | all-reduce | flops 9216 | bytes 73728 | tf_op jit(solution)/shard_map/psum | solution.py:262
  632.5 34.3 %reduce-scatter.19.cloned.1.call-done = bf16[768,768]{1,0:T(8,128)(2,1)} async-done(((bf16[768,3072]{1,0:T(8,128)(2,1)}), bf16[768,768]{1,0:T(8,128)(2,1)}) %reduce-scatter.19.cloned.1.call-update) | async-done | bytes 1179664 | tf_op jit(solution)/shard_map/reduce_scatter | solution.py:136
  673.4 30.7 %reduce-scatter.27.cloned.1.call-done = bf16[96,192]{1,0:T(8,128)(2,1)} async-done(((bf16[768,192]{1,0:T(8,128)(2,1)}), bf16[96,192]{1,0:T(8,128)(2,1)}) %reduce-scatter.27.cloned.1.call-update) | async-done | bytes 36880
  706.7 37.3 %reduce-scatter.15.cloned.1.call-done = bf16[3,96,192]{2,1,0:T(8,128)(2,1)} async-done(((bf16[3,768,192]{2,1,0:T(8,128)(2,1)}), bf16[3,96,192]{2,1,0:T(8,128)(2,1)}) %reduce-scatter.15.cloned.1.call-update) | async-done | bytes 110608 | tf_op jit(solution)/shard_map/reduce_scatter | solution.py:139
  746.1 38.2 %reduce-scatter.29.cloned.1.call-done = bf16[96,768]{1,0:T(8,128)(2,1)} async-done(((bf16[768,768]{1,0:T(8,128)(2,1)}), bf16[96,768]{1,0:T(8,128)(2,1)}) %reduce-scatter.29.cloned.1.call-update) | async-done | bytes 147472
  786.6 37.6 %reduce-scatter.21.cloned.1.call-done = bf16[96,768]{1,0:T(8,128)(2,1)} async-done(((bf16[768,768]{1,0:T(8,128)(2,1)}), bf16[96,768]{1,0:T(8,128)(2,1)}) %reduce-scatter.21.cloned.1.call-update) | async-done | bytes 147472 | tf_op jit(solution)/shard_map/reduce_scatter | solution.py:139
  (220 shorter events, 99.4 us)
Async XLA Ops:
  7.2 33.3 %all-gather.12.cloned.1.call-start = ((), (), s32[]{:S(2)}) async-start(), calls=%async_computation.10 | async-start | bytes 1327104 | tf_op jit(solution)/shard_map/all_gather | solution.py:132
  8.9 57.5 %all-gather.16.cloned.1.call-start = ((), (), s32[]{:S(2)}) async-start(), calls=%async_computation.12 | async-start | bytes 1327104 | tf_op jit(solution)/shard_map/all_gather | solution.py:132
  10.6 127.9 %all-gather.8.cloned.1.call-start = ((), (), s32[]{:S(2)}) async-start(), calls=%async_computation.8 | async-start | bytes 4423680 | tf_op jit(solution)/shard_map/all_gather | solution.py:133
  30.1 139.6 %all-gather.10.cloned.1.call-start = ((), (), s32[]{:S(2)}) async-start(), calls=%async_computation.9 | async-start | bytes 1474560 | tf_op jit(solution)/shard_map/all_gather | solution.py:133
  40.4 219.2 %all-gather.14.cloned.1.call-start = ((), (), s32[]{:S(2)}) async-start(), calls=%async_computation.11 | async-start | bytes 5898240 | tf_op jit(solution)/shard_map/all_gather | solution.py:133
  41.0 307.9 %all-gather.18.cloned.1.call-start = ((), (), s32[]{:S(2)}) async-start(), calls=%async_computation.13 | async-start | bytes 5898240 | tf_op jit(solution)/shard_map/all_gather | solution.py:133
  54.9 294.0 %copy-start.42 = (f32[768]{0:T(1024)}, f32[768]{0:T(1024)S(1)}, u32[]{:S(2)}) copy-start(f32[768]{0:T(1024)S(1)} %get-tuple-element.179) | copy-start | bytes 9220
  54.9 315.6 %copy-start.30 = (f32[768]{0:T(1024)}, f32[768]{0:T(1024)S(1)}, u32[]{:S(2)}) copy-start(f32[768]{0:T(1024)S(1)} %get-tuple-element.180) | copy-start | bytes 9220
  66.4 375.1 %reduce-scatter.17.cloned.1.call-start = ((), (), s32[]{:S(2)}) async-start(), calls=%async_computation.15 | async-start | bytes 1474560 | tf_op jit(solution)/shard_map/reduce_scatter | solution.py:136
  172.3 194.5 %copy-start.7 = (f32[512,768]{1,0:T(8,128)}, f32[512,768]{1,0:T(8,128)S(1)}, u32[]{:S(2)}) copy-start(f32[512,768]{1,0:T(8,128)S(1)} %get-tuple-element.215) | copy-start | bytes 4718596
  172.6 197.9 %copy-start.35 = (f32[512]{0:T(512)}, f32[512]{0:T(512)S(1)}, u32[]{:S(2)}) copy-start(f32[512]{0:T(512)S(1)} %fusion.39) | copy-start | bytes 6148
  379.9 109.9 %reduce-scatter.25.cloned.1.call-start = ((), (), s32[]{:S(2)}) async-start(), calls=%async_computation.19 | async-start | bytes 4423680
  425.1 152.6 %reduce-scatter.23.cloned.1.call-start = ((), (), s32[]{:S(2)}) async-start(), calls=%async_computation.18 | async-start | bytes 5898240 | tf_op jit(solution)/shard_map/reduce_scatter | solution.py:136
  433.3 233.4 %reduce-scatter.19.cloned.1.call-start = ((), (), s32[]{:S(2)}) async-start(), calls=%async_computation.16 | async-start | bytes 5898240 | tf_op jit(solution)/shard_map/reduce_scatter | solution.py:136
  441.5 262.6 %reduce-scatter.27.cloned.1.call-start = ((), (), s32[]{:S(2)}) async-start(), calls=%async_computation.20 | async-start | bytes 442368
  443.5 300.5 %reduce-scatter.15.cloned.1.call-start = ((), (), s32[]{:S(2)}) async-start(), calls=%async_computation.14 | async-start | bytes 1327104 | tf_op jit(solution)/shard_map/reduce_scatter | solution.py:139
  492.9 87.3 %copy-start.40 = (f32[768]{0:T(1024)S(1)}, f32[768]{0:T(1024)}, u32[]{:S(2)}) copy-start(f32[768]{0:T(1024)} %get-tuple-element.175) | copy-start | bytes 9220
  492.9 87.3 %copy-start.4 = (f32[512,768]{1,0:T(8,128)S(1)}, f32[512,768]{1,0:T(8,128)}, u32[]{:S(2)}) copy-start(f32[512,768]{1,0:T(8,128)} %copy-done.3) | copy-start | bytes 4718596
  496.5 287.8 %reduce-scatter.29.cloned.1.call-start = ((), (), s32[]{:S(2)}) async-start(), calls=%async_computation.21 | async-start | bytes 1327104
  580.1 244.1 %reduce-scatter.21.cloned.1.call-start = ((), (), s32[]{:S(2)}) async-start(), calls=%async_computation.17 | async-start | bytes 1327104 | tf_op jit(solution)/shard_map/reduce_scatter | solution.py:139
  673.4 150.9 %copy-start.14 = (f32[96,768]{1,0:T(8,128)S(1)}, f32[96,768]{1,0:T(8,128)}, u32[]{:S(2)}) copy-start(f32[96,768]{1,0:T(8,128)} %param.30) | copy-start | bytes 884740
  673.4 150.9 %copy-start.20 = (f32[96,768]{1,0:T(8,128)S(1)}, f32[96,768]{1,0:T(8,128)}, u32[]{:S(2)}) copy-start(f32[96,768]{1,0:T(8,128)} %param.31) | copy-start | bytes 884740
  673.4 150.9 %copy-start.21 = (f32[96,768]{1,0:T(8,128)S(1)}, f32[96,768]{1,0:T(8,128)}, u32[]{:S(2)}) copy-start(f32[96,768]{1,0:T(8,128)} %param.32) | copy-start | bytes 884740
  704.1 122.1 %copy-start.1 = (s32[4,512]{1,0:T(4,128)S(1)}, s32[4,512]{1,0:T(4,128)}, u32[]{:S(2)}) copy-start(s32[4,512]{1,0:T(4,128)} %param.23) | copy-start | bytes 24580
  (44 other events, 1119.1 us)
Sparse Core Ops, SparseCore 0:
  10.5 29.4 all-gather.11
  42.5 23.8 all-gather.15
  68.5 69.9 all-gather.7
  140.5 29.0 all-gather.9
  171.0 88.5 all-gather.13
  261.0 87.8 all-gather.17
  380.0 27.5 reduce-scatter.16
  425.2 64.5 reduce-scatter.24
  492.1 85.5 reduce-scatter.22
  579.9 86.8 reduce-scatter.18
  669.8 34.2 reduce-scatter.26
  707.2 36.7 reduce-scatter.14
  747.5 36.7 reduce-scatter.28
  787.4 36.7 reduce-scatter.20

commit v2 on v1

--- a/solution.py
+++ b/solution.py
@@ -4,6 +4,8 @@
 import jax
 import jax.numpy as jnp
 from jax import lax
+from jax.experimental import pallas as pl
+from jax.experimental.pallas import tpu as pltpu
 from jax.sharding import PartitionSpec as P
 
 DH = 64
@@ -298,9 +300,719 @@
     )
 
 
+F32 = jnp.float32
+BF16 = jnp.bfloat16
+MESH = pl.DeviceIdType.MESH
+PLANES = 4
+CHIPS = 4
+TILE = 256
+SLOTS_HELD = 5
+LENT = 4
+
+
+def mm(left, right):
+    return lax.dot_general(left, right, (((1,), (0,)), ((), ())), preferred_element_type=F32)
+
+
+def mm_nt(left, right):
+    return lax.dot_general(left, right, (((1,), (1,)), ((), ())), preferred_element_type=F32)
+
+
+def mm_tn(left, right):
+    return lax.dot_general(left, right, (((0,), (0,)), ((), ())), preferred_element_type=F32)
+
+
+def gelu_parts(u):
+    tail = jnp.exp(u * u * -0.5)
+    t = 1.0 / (1.0 + (0.3275911 * math.sqrt(0.5)) * jnp.abs(u))
+    poly = 1.061405429 * t - 1.453152027
+    poly = poly * t + 1.421413741
+    poly = poly * t - 0.284496736
+    poly = poly * t + 0.254829592
+    upper = (0.5 * t) * poly * tail
+    cdf = jnp.where(u < 0.0, upper, 1.0 - upper)
+    return cdf, cdf + u * tail * (1.0 / math.sqrt(2.0 * math.pi))
+
+
+def layer_kernel(
+    tokens_hbm, cot_ref, seg_ref, pack_ref, bias_ref, vec_ref,
+    block_ref, tgrad_ref, grad_ref, small_ref,
+    W, TOK, XT, XT2, QKV, ATT, PT, PRE, RSTD, NB, PO, HID, GP, GB, DHP,
+    BIAS, MASK, G, SR, DR, PR, ZR, SMK, SMS, SMR, SMZ,
+    gather_send, gather_recv, red_send, red_recv, small_send, small_recv, bias_send, bias_recv,
+    local_sem, credit_sem,
+):
+    dp = lax.axis_index("dp")
+    z = lax.axis_index("tensor")
+    core = dp % 2
+    chip = dp // 2
+    jx = (chip // 2) * 2 + (1 - chip % 2)
+    jy = (1 - chip // 2) * 2 + chip % 2
+    jd = 3 - chip
+    n_tok = TOK.shape[0]
+    width = TOK.shape[1]
+    rows = pack_ref.shape[1]
+    half = rows // 2
+    dev_sib = (chip * 2 + (1 - core), z)
+    dev_x = (jx * 2 + core, z)
+    dev_y = (jy * 2 + core, z)
+
+    def plane(k):
+        return (z + k) % PLANES
+
+    def dev_z(k):
+        return (dp, plane(k))
+
+    def rd(j, c, start=0, size=rows):
+        return pl.ds(pl.multiple_of((2 * j + c) * rows + start, 16), size)
+
+    def remote(src, dst, ssem, rsem, dev):
+        return pltpu.make_async_remote_copy(
+            src_ref=src, dst_ref=dst, send_sem=ssem, recv_sem=rsem, device_id=dev, device_id_type=MESH
+        )
+
+    tok_copy = pltpu.make_async_copy(
+        tokens_hbm.at[pl.ds(pl.multiple_of(z * n_tok, 16), n_tok)], TOK, local_sem
+    )
+    tok_copy.start()
+    for m in range(3):
+        W[m, z, rd(chip, core), :] = pack_ref[m]
+    BIAS[z] = bias_ref[...]
+
+    barrier = pltpu.get_barrier_semaphore()
+    for dev in (dev_sib, dev_x, dev_y, dev_z(1), dev_z(2), dev_z(3)):
+        pl.semaphore_signal(barrier, inc=1, device_id=dev, device_id_type=MESH)
+    pl.semaphore_wait(barrier, 6)
+
+    def send_block(m, t, j, c, kind, dev, start=0, size=rows):
+        region = W.at[m, t, rd(j, c, start, size)]
+        return remote(region, region, gather_send.at[m, kind], gather_recv.at[m, kind], dev)
+
+    def wait_block(m, t, j, c, kind, start=0, size=rows):
+        region = W.at[m, t, rd(j, c, start, size)]
+        remote(region, region, gather_send.at[m, kind], gather_recv.at[m, kind], dev_sib).wait_recv()
+
+    def z_sends(m):
+        for k in (1, 2, 3):
+            send_block(m, z, chip, core, k - 1, dev_z(PLANES - k)).start()
+
+    def first(m, k):
+        t = plane(k)
+
+        @pl.when(k > 0)
+        def _():
+            wait_block(m, t, chip, core, k - 1)
+
+        send_block(m, t, chip, core, 3 + k, dev_x).start()
+        send_block(m, t, chip, core, 7 + k, dev_y).start()
+        send_block(m, t, chip, core, 19 + k, dev_sib).start()
+
+    def second(m, k):
+        t = plane(k)
+        wait_block(m, t, jx, core, 3 + k)
+        send_block(m, t, jx, core, 15 + k, dev_y, 0, half).start()
+        wait_block(m, t, jy, core, 7 + k)
+        send_block(m, t, jy, core, 11 + k, dev_x, half, half).start()
+        send_block(m, t, jx, core, 23 + k, dev_sib).start()
+        send_block(m, t, jy, core, 27 + k, dev_sib).start()
+
+    def third(m, k):
+        t = plane(k)
+        wait_block(m, t, jd, core, 15 + k, 0, half)
+        wait_block(m, t, jd, core, 11 + k, half, half)
+        send_block(m, t, jd, core, 31 + k, dev_sib).start()
+        wait_block(m, t, chip, 1 - core, 19 + k)
+        wait_block(m, t, jx, 1 - core, 23 + k)
+        wait_block(m, t, jy, 1 - core, 27 + k)
+        wait_block(m, t, jd, 1 - core, 31 + k)
+
+    def gather_step(i):
+        @pl.when(i < 10)
+        def _():
+            nxt = i + 2
+            m, k = nxt // PLANES, nxt % PLANES
+            first(m, k)
+
+            @pl.when((k == 1) & (m < 2))
+            def _():
+                z_sends(m + 1)
+
+        @pl.when(i < 11)
+        def _():
+            nxt = i + 1
+            second(nxt // PLANES, nxt % PLANES)
+
+        third(i // PLANES, i % PLANES)
+
+    z_sends(0)
+    for k in (1, 2, 3):
+        remote(
+            BIAS.at[z], BIAS.at[z], bias_send.at[k - 1], bias_recv.at[k - 1], dev_z(PLANES - k)
+        ).start()
+    first(0, 0)
+    tok_copy.wait()
+    first(0, 1)
+    z_sends(1)
+    second(0, 0)
+
+    vec = vec_ref[...]
+
+    @pl.loop(0, 8)
+    def _(r):
+        part = pl.ds(pl.multiple_of(r * (n_tok // 8), 16), n_tok // 8)
+        PRE[part, :] = TOK[part, :].astype(F32) + vec[0:1]
+
+    seg_row = seg_ref[pl.ds(z, 1), :].astype(F32)
+    seg_col = jnp.broadcast_to(seg_row, (128, n_tok)).T
+    span = 3 * n_tok // 4
+    for b in range(2):
+        keys = seg_col[128 * b : 128 * b + span, 0:1]
+        queries = seg_row[:, 256 * b : 256 * b + 256]
+        MASK[b] = jnp.where(keys == queries, 0.0, NEG_FILL)
+
+    for k in (1, 2, 3):
+        remote(
+            BIAS.at[plane(k)], BIAS.at[plane(k)], bias_send.at[k - 1], bias_recv.at[k - 1], dev_sib
+        ).wait_recv()
+
+    lane = lax.broadcasted_iota(jnp.int32, (1, width), 1)
+    q_scale = jnp.where(lane < 3 * DH, 1.0 / math.sqrt(DH), 1.0)
+    heads = 3
+    local = heads * DH
+
+    def forward_attention(k):
+        t = plane(k)
+        for n in range(3):
+            cols = slice(n * TILE, (n + 1) * TILE)
+            res = mm(TOK[...], W[0, t, :, cols]) + BIAS[t, 0:1, cols]
+            QKV[k, :, cols] = (res * q_scale[:, cols]).astype(BF16)
+        attended = []
+        for h in range(heads):
+            query = QKV[k, :, h * DH : (h + 1) * DH]
+            keys = QKV[k, :, local + h * DH : local + (h + 1) * DH]
+            values = QKV[k, :, 3 * local + h * DH : 3 * local + (h + 1) * DH]
+            outs = []
+            for b in range(2):
+                scores = mm_nt(
+                    keys[128 * b : 128 * b + span], query[256 * b : 256 * b + 256]
+                ) + MASK[b]
+                terms = jnp.exp(scores - jnp.max(scores, axis=0, keepdims=True))
+                total = jnp.sum(terms, axis=0, keepdims=True)
+                soft = (terms * (1.0 / total)).astype(BF16)
+                PT[k, h, b] = soft
+                outs.append(mm_tn(soft, values[128 * b : 128 * b + span]))
+            attended.append(jnp.concatenate(outs, axis=0))
+        out = jnp.concatenate(attended, axis=1).astype(BF16)
+        ATT[k] = out
+        for n in range(3):
+            cols = slice(n * TILE, (n + 1) * TILE)
+            PRE[:, cols] += mm_nt(out, W[0, t, cols, 2 * local : 3 * local])
+
+    def forward_norm():
+        @pl.loop(0, 8)
+        def _(r):
+            part = pl.ds(pl.multiple_of(r * (n_tok // 8), 16), n_tok // 8)
+            rows_in = PRE[part, :]
+            centered = rows_in - jnp.mean(rows_in, axis=-1, keepdims=True)
+            scale = lax.rsqrt(jnp.mean(centered * centered, axis=-1, keepdims=True) + NORM_EPS)
+            unit = centered * scale
+            PRE[part, :] = unit
+            RSTD[part, :] = jnp.broadcast_to(scale, (n_tok // 8, 128))
+            normed = unit * vec[1:2] + vec[2:3]
+            NB[part, :] = normed.astype(BF16)
+            PO[part, :] = normed + vec[3:4]
+
+    def forward_up(k):
+        t = plane(k)
+        for n in range(3):
+            cols = slice(n * TILE, (n + 1) * TILE)
+            u = mm(NB[...], W[1, t, :, cols]) + BIAS[t, 1:2, cols]
+            cdf, slope = gelu_parts(u)
+            HID[k, :, cols] = (u * cdf).astype(BF16)
+            GP[k, :, cols] = slope.astype(BF16)
+
+    def forward_down(k):
+        t = plane(k)
+        for n in range(3):
+            cols = slice(n * TILE, (n + 1) * TILE)
+            PO[:, cols] += mm_nt(HID[k], W[2, t, cols, :])
+
+    for p, work in enumerate((forward_attention, forward_up, forward_down)):
+
+        @pl.loop(0, PLANES)
+        def _(k, p=p, work=work):
+            gather_step(p * PLANES + k)
+            work(k)
+
+        if p == 0:
+            forward_norm()
+
+    SMK[...] = jnp.zeros_like(SMK)
+    SMS[...] = jnp.zeros_like(SMS)
+
+    @pl.loop(0, 8)
+    def _(r):
+        part = pl.ds(pl.multiple_of(r * (n_tok // 8), 16), n_tok // 8)
+        rows_in = PO[part, :]
+        centered = rows_in - jnp.mean(rows_in, axis=-1, keepdims=True)
+        scale = lax.rsqrt(jnp.mean(centered * centered, axis=-1, keepdims=True) + NORM_EPS)
+        unit = centered * scale
+        block_ref[part, :] = (unit * vec[4:5] + vec[5:6]).astype(BF16)
+        cot = cot_ref[part, :].astype(F32)
+        e = cot * vec[4:5]
+        grad = scale * (
+            e
+            - jnp.mean(e, axis=-1, keepdims=True)
+            - unit * jnp.mean(e * unit, axis=-1, keepdims=True)
+        )
+        PO[part, :] = grad
+        GB[part, :] = grad.astype(BF16)
+        SMS[11:12, :] += jnp.sum(grad, axis=0, keepdims=True)
+        SMS[12:13, :] += jnp.sum(cot * unit, axis=0, keepdims=True)
+        SMS[13:14, :] += jnp.sum(cot, axis=0, keepdims=True)
+
+    def unit_rows(j, start=0, size=rows):
+        return pl.ds(pl.multiple_of(j * rows + start, 16), size)
+
+    def red(src, dst, u, stage, dev):
+        return remote(src, dst, red_send.at[u, stage], red_recv.at[u, stage], dev)
+
+    def held(u, j, start=0, size=rows):
+        return G.at[u % SLOTS_HELD, core, unit_rows(j, start, size)]
+
+    def to_sibling(u):
+        return red(G.at[u % SLOTS_HELD, 1 - core], SR.at[u % LENT], u, 0, dev_sib)
+
+    def relay_y(u):
+        return red(held(u, jd, 0, half), DR.at[u, 0], u, 1, dev_y)
+
+    def relay_x(u):
+        return red(held(u, jd, half, half), DR.at[u, 1], u, 2, dev_x)
+
+    def along_x(u):
+        return red(held(u, jx), PR.at[u, 0], u, 3, dev_x)
+
+    def along_y(u):
+        return red(held(u, jy), PR.at[u, 1], u, 4, dev_y)
+
+    def along_z(u):
+        kk = u % PLANES
+        return red(held(u, chip), ZR.at[u // PLANES, kk], u, 5, (dp, (z + 1 + kk) % PLANES))
+
+    def step_one(u):
+        @pl.when(u >= LENT)
+        def _():
+            pl.semaphore_wait(credit_sem, 1)
+
+        to_sibling(u).start()
+
+    def step_two(u):
+        to_sibling(u).wait_recv()
+
+        def merge(j):
+            here = unit_rows(j)
+            slot = u % SLOTS_HELD
+            both = G[slot, core, here, :].astype(F32) + SR[u % LENT, here, :].astype(F32)
+            G[slot, core, here, :] = both.astype(BF16)
+
+        merge(jd)
+        relay_y(u).start()
+        relay_x(u).start()
+        merge(jx)
+        merge(jy)
+        merge(chip)
+
+        @pl.when(u < 12 - LENT)
+        def _():
+            pl.semaphore_signal(credit_sem, inc=1, device_id=dev_sib, device_id_type=MESH)
+
+    def step_three(u):
+        slot = u % SLOTS_HELD
+        relay_y(u).wait_recv()
+        here = unit_rows(jx, 0, half)
+        G[slot, core, here, :] = (
+            G[slot, core, here, :].astype(F32) + DR[u, 0].astype(F32)
+        ).astype(BF16)
+        along_x(u).start()
+        relay_x(u).wait_recv()
+        here = unit_rows(jy, half, half)
+        G[slot, core, here, :] = (
+            G[slot, core, here, :].astype(F32) + DR[u, 1].astype(F32)
+        ).astype(BF16)
+        along_y(u).start()
+
+    def step_four(u):
+        slot = u % SLOTS_HELD
+        along_x(u).wait_recv()
+        along_y(u).wait_recv()
+        here = unit_rows(chip)
+        own = (
+            G[slot, core, here, :].astype(F32) + PR[u, 0].astype(F32) + PR[u, 1].astype(F32)
+        )
+
+        @pl.when(u % PLANES < PLANES - 1)
+        def _():
+            G[slot, core, here, :] = own.astype(BF16)
+            along_z(u).start()
+
+        @pl.when(u % PLANES == PLANES - 1)
+        def _():
+            grad_ref[u // PLANES] = own
+
+    def sends_done(u):
+        to_sibling(u).wait_send()
+        relay_y(u).wait_send()
+        relay_x(u).wait_send()
+        along_x(u).wait_send()
+        along_y(u).wait_send()
+
+        @pl.when(u % PLANES < PLANES - 1)
+        def _():
+            along_z(u).wait_send()
+
+    def reduce_step(u):
+        @pl.when(u < 12)
+        def _():
+            step_one(u)
+
+        @pl.when((u >= 1) & (u < 13))
+        def _():
+            step_two(u - 1)
+
+        @pl.when((u >= 2) & (u < 14))
+        def _():
+            step_three(u - 2)
+
+        @pl.when((u >= 3) & (u < 15))
+        def _():
+            step_four(u - 3)
+
+    def before_unit(u):
+        @pl.when(u >= SLOTS_HELD)
+        def _():
+            sends_done(u - SLOTS_HELD)
+
+    def transposed(src, dst):
+        for j in range(CHIPS):
+            for c in range(2):
+                lo = (2 * j + c) * rows
+                dst[c, j * rows : (j + 1) * rows, :] = src[:, lo : lo + rows].T
+
+    def fill(u, left, right_of, lo, hi):
+        slot = u % SLOTS_HELD
+        for c in range(2):
+            G[slot, c, :, lo:hi] = mm(left[c], right_of(lo, hi)).astype(BF16)
+
+    transposed(GB, XT)
+
+    def backward_down(u, k):
+        for n in range(3):
+            fill(u, XT, lambda lo, hi: HID[k, :, lo:hi], n * TILE, (n + 1) * TILE)
+
+    def backward_up(u, k):
+        t = plane(k)
+        for n in range(3):
+            cols = slice(n * TILE, (n + 1) * TILE)
+            grad = mm(GB[...], W[2, t, :, cols]) * GP[k, :, cols].astype(F32)
+            low = grad.astype(BF16)
+            DHP[:, cols] = low
+            SMK[t, 1:2, cols] = jnp.sum(low.astype(F32), axis=0, keepdims=True)
+        for n in range(3):
+            fill(u, XT, lambda lo, hi: DHP[:, lo:hi], n * TILE, (n + 1) * TILE)
+        for n in range(3):
+            cols = slice(n * TILE, (n + 1) * TILE)
+            PO[:, cols] += mm_nt(DHP[...], W[1, t, cols, :])
+
+    def backward_norm():
+        @pl.loop(0, 8)
+        def _(r):
+            part = pl.ds(pl.multiple_of(r * (n_tok // 8), 16), n_tok // 8)
+            grad_in = PO[part, :]
+            unit = PRE[part, :]
+            e = grad_in * vec[1:2]
+            grad = RSTD[part, 0:1] * (
+                e
+                - jnp.mean(e, axis=-1, keepdims=True)
+                - unit * jnp.mean(e * unit, axis=-1, keepdims=True)
+            )
+            tgrad_ref[part, :] = grad
+            GB[part, :] = grad.astype(BF16)
+            SMS[8:9, :] += jnp.sum(grad, axis=0, keepdims=True)
+            SMS[9:10, :] += jnp.sum(grad_in * unit, axis=0, keepdims=True)
+            SMS[10:11, :] += jnp.sum(grad_in, axis=0, keepdims=True)
+
+    def backward_attention(u, k):
+        t = plane(k)
+        back = mm(GB[...], W[0, t, :, 2 * local : 3 * local]).astype(BF16)
+        grads = ([], [], [])
+        for h in range(heads):
+            query = QKV[k, :, h * DH : (h + 1) * DH]
+            keys = QKV[k, :, local + h * DH : local + (h + 1) * DH]
+            values = QKV[k, :, 3 * local + h * DH : 3 * local + (h + 1) * DH]
+            d_out = back[:, h * DH : (h + 1) * DH]
+            d_query, d_keys, d_values = [], [], []
+            for b in range(2):
+                win = slice(128 * b, 128 * b + span)
+                blk = slice(256 * b, 256 * b + 256)
+                soft = PT[k, h, b]
+                wide = soft.astype(F32)
+                d_soft = mm_nt(values[win], d_out[blk])
+                inner = jnp.sum(wide * d_soft, axis=0, keepdims=True)
+                d_scores = (wide * (d_soft - inner)).astype(BF16)
+                d_query.append(mm_tn(d_scores, keys[win]))
+                d_keys.append(mm(d_scores, query[blk]))
+                d_values.append(mm(soft, d_out[blk]))
+
+            def overlap(pair):
+                return jnp.concatenate(
+                    [pair[0][:128], pair[0][128:] + pair[1][:256], pair[1][256:]], axis=0
+                )
+
+            grads[0].append(jnp.concatenate(d_query, axis=0) * (1.0 / math.sqrt(DH)))
+            grads[1].append(overlap(d_keys))
+            grads[2].append(overlap(d_values))
+        empty = jnp.zeros((n_tok, local), F32)
+        DHP[...] = jnp.concatenate(
+            grads[0] + grads[1] + [empty] + grads[2], axis=1
+        ).astype(BF16)
+        SMK[t, 0:1, :] = jnp.sum(DHP[...].astype(F32), axis=0, keepdims=True)
+        fill(u, XT, lambda lo, hi: DHP[:, lo:hi], 0, 2 * local)
+        fill(u, XT2, lambda lo, hi: ATT[k], 2 * local, 3 * local)
+        fill(u, XT, lambda lo, hi: DHP[:, lo:hi], 3 * local, 4 * local)
+        for n in range(3):
+            cols = slice(n * TILE, (n + 1) * TILE)
+            tgrad_ref[:, cols] += mm_nt(DHP[...], W[0, t, cols, :])
+
+    for p, work in enumerate((backward_down, backward_up, backward_attention)):
+
+        @pl.loop(0, PLANES)
+        def _(kk, p=p, work=work):
+            u = p * PLANES + kk
+            before_unit(u)
+            work(u, (kk + 1) % PLANES)
+            reduce_step(u)
+
+        if p == 0:
+            transposed(NB, XT)
+        if p == 1:
+            backward_norm()
+            transposed(TOK, XT)
+            transposed(GB, XT2)
+
+    for t in range(PLANES):
+        SMS[2 * t : 2 * t + 2, :] = SMK[t, 0:2, :]
+
+    def small(step, dev):
+        return remote(SMS, SMR.at[step], small_send.at[step], small_recv.at[step], dev)
+
+    for step, dev in enumerate((dev_sib, dev_x, dev_y)):
+        reduce_step(12 + step)
+        copy = small(step, dev)
+        copy.start()
+        copy.wait()
+        SMS[...] += SMR[step]
+
+    SMZ[z] = SMS[...]
+
+    def small_z(k, dev):
+        return remote(SMS, SMZ.at[z], small_send.at[2 + k], small_recv.at[2 + k], dev)
+
+    for k in (1, 2, 3):
+        small_z(k, dev_z(PLANES - k)).start()
+    for k in (1, 2, 3):
+        remote(
+            SMS, SMZ.at[plane(k)], small_send.at[2 + k], small_recv.at[2 + k], dev_sib
+        ).wait_recv()
+    small_ref[...] = (SMZ[0] + SMZ[1]) + (SMZ[2] + SMZ[3])
+
+    for p in range(3):
+        total = grad_ref[p]
+        for kk in range(3):
+            remote(
+                ZR.at[p, kk], ZR.at[p, kk], red_send.at[4 * p + kk, 5],
+                red_recv.at[4 * p + kk, 5], dev_sib,
+            ).wait_recv()
+            total = total + ZR[p, kk].astype(F32)
+        grad_ref[p] = total
+
+    for k in (1, 2, 3):
+        small_z(k, dev_z(PLANES - k)).wait_send()
+        remote(
+            BIAS.at[z], BIAS.at[z], bias_send.at[k - 1], bias_recv.at[k - 1], dev_z(PLANES - k)
+        ).wait_send()
+
+    @pl.loop(12 - SLOTS_HELD, 12)
+    def _(u):
+        sends_done(u)
+
+    @pl.loop(0, 3)
+    def _(m):
+        for k in (1, 2, 3):
+            send_block(m, z, chip, core, k - 1, dev_z(PLANES - k)).wait_send()
+
+        @pl.loop(0, PLANES)
+        def _(k):
+            t = plane(k)
+            send_block(m, t, chip, core, 3 + k, dev_x).wait_send()
+            send_block(m, t, chip, core, 7 + k, dev_y).wait_send()
+            send_block(m, t, jx, core, 15 + k, dev_y, 0, half).wait_send()
+            send_block(m, t, jy, core, 11 + k, dev_x, half, half).wait_send()
+            for kind in (19, 23, 27, 31):
+                send_block(m, t, chip, core, kind + k, dev_sib).wait_send()
+
+
+def run_layer(tokens, cotangent, segment_ids, packs, bias_rows, vectors):
+    n_tok = cotangent.shape[0]
+    width = tokens.shape[1]
+    rows = packs.shape[1]
+    span = 3 * n_tok // 4
+    vmem = pl.BlockSpec(memory_space=pltpu.VMEM)
+    low = lambda *shape: pltpu.VMEM(shape, BF16)
+    wide = lambda *shape: pltpu.VMEM(shape, F32)
+    dma = lambda *shape: pltpu.SemaphoreType.DMA(shape)
+    return pl.pallas_call(
+        layer_kernel,
+        name="encoder_layer",
+        out_shape=(
+            jax.ShapeDtypeStruct((n_tok, width), BF16),
+            jax.ShapeDtypeStruct((n_tok, width), F32),
+            jax.ShapeDtypeStruct((3, rows, width), F32),
+            jax.ShapeDtypeStruct((16, width), F32),
+        ),
+        in_specs=[pl.BlockSpec(memory_space=pl.ANY)] + [vmem] * 5,
+        out_specs=(vmem,) * 4,
+        scratch_shapes=[
+            low(3, PLANES, width, width),
+            low(n_tok, width),
+            low(2, CHIPS * rows, n_tok),
+            low(2, CHIPS * rows, n_tok),
+            low(PLANES, n_tok, width),
+            low(PLANES, n_tok, 3 * DH),
+            low(PLANES, 3, 2, span, n_tok // 2),
+            wide(n_tok, width),
+            wide(n_tok, 128),
+            low(n_tok, width),
+            wide(n_tok, width),
+            low(PLANES, n_tok, width),
+            low(PLANES, n_tok, width),
+            low(n_tok, width),
+            low(n_tok, width),
+            wide(PLANES, 8, width),
+            wide(2, span, n_tok // 2),
+            low(SLOTS_HELD, 2, CHIPS * rows, width),
+            low(LENT, CHIPS * rows, width),
+            low(12, 2, rows // 2, width),
+            low(12, 2, rows, width),
+            low(3, 3, rows, width),
+            wide(PLANES, 8, width),
+            wide(16, width),
+            wide(3, 16, width),
+            wide(PLANES, 16, width),
+            dma(3, 35),
+            dma(3, 35),
+            dma(12, 6),
+            dma(12, 6),
+            dma(6),
+            dma(6),
+            dma(3),
+            dma(3),
+            pltpu.SemaphoreType.DMA,
+            pltpu.SemaphoreType.REGULAR,
+        ],
+        compiler_params=pltpu.CompilerParams(
+            collective_id=0, has_side_effects=True, vmem_limit_bytes=63 * 2**20
+        ),
+    )(tokens, cotangent, segment_ids, packs, bias_rows, vectors)
+
+
+def on_device_whole(
+    tokens, cotangent, segment_ids,
+    input_weight, input_first, input_second,
+    output_weight, output_first, output_second,
+    up_weight, up_first, up_second,
+    down_weight, down_first, down_second,
+    inner_bias, inner_first, inner_second,
+    vectors, vector_first, vector_second,
+):
+    rows, local_width = input_weight.shape[1:]
+    width = tokens.shape[1]
+    local = 3 * DH
+    low = lambda v: v.astype(BF16)
+    pack_a = jnp.concatenate(
+        [
+            low(input_weight[0]), low(input_weight[1]), low(output_weight).T, low(input_weight[2])
+        ],
+        axis=1,
+    )
+    packs = jnp.stack([pack_a, low(up_weight), low(down_weight).T])
+    none = jnp.zeros((local_width,), F32)
+    bias_rows = jnp.concatenate(
+        [
+            jnp.concatenate([inner_bias[0], none, none, inner_bias[1]])[None],
+            inner_bias[2:].T.reshape(1, -1),
+            jnp.zeros((6, width), F32),
+        ],
+        axis=0,
+    )
+    vec_rows = jnp.concatenate([vectors, jnp.zeros((2, width), F32)], axis=0)
+    block_out, token_grad, shard_grads, small = run_layer(
+        tokens, cotangent, segment_ids, packs, bias_rows, vec_rows
+    )
+    input_shard = jnp.stack(
+        [
+            shard_grads[2, :, :local],
+            shard_grads[2, :, local : 2 * local],
+            shard_grads[2, :, 3 * local :],
+        ]
+    )
+    output_shard = shard_grads[2, :, 2 * local : 3 * local].T
+    up_shard = shard_grads[1]
+    down_shard = shard_grads[0].T
+    own = lax.dynamic_slice_in_dim(small, 2 * lax.axis_index("tensor"), 2, 0)
+    inner_grad = jnp.concatenate(
+        [own[0:1, :local], own[0:1, 3 * local :], own[1].reshape(local, 4).T], axis=0
+    )
+    vector_sum = small[8:14]
+    new_input = adam_update(
+        input_weight, input_first, input_second, input_shard, RATE_INPUT, WEIGHT_DECAY
+    )
+    new_output = adam_update(
+        output_weight, output_first, output_second, output_shard, RATE_OUTPUT, WEIGHT_DECAY
+    )
+    new_up = adam_update(up_weight, up_first, up_second, up_shard, RATE_UP, WEIGHT_DECAY)
+    new_down = adam_update(
+        down_weight, down_first, down_second, down_shard, RATE_DOWN, WEIGHT_DECAY
+    )
+    new_inner = adam_update(inner_bias, inner_first, inner_second, inner_grad, RATE_VECTOR, 0.0)
+    new_vector = adam_update(vectors, vector_first, vector_second, vector_sum, RATE_OUTER, 0.0)
+    return (
+        block_out,
+        token_grad,
+        new_input[0],
+        new_input[1],
+        new_input[2],
+        new_output[0],
+        new_output[1],
+        new_output[2],
+        new_up[0],
+        new_up[1],
+        new_up[2],
+        new_down[0],
+        new_down[1],
+        new_down[2],
+        new_inner[0],
+        new_inner[1],
+        new_inner[2],
+        new_vector[0],
+        new_vector[1],
+        new_vector[2],
+    )
+
+
 def solution(mesh):
+    whole = mesh.shape["dp"] == 2 * CHIPS and mesh.shape["tensor"] == PLANES
     return jax.shard_map(
-        on_device,
+        on_device_whole if whole else on_device,
         mesh=mesh,
         in_specs=(
             P("dp", None),

time: 842 us -> 193 us (0.23); the launches traced: 833 us -> 193 us
  waiting for transfers between devices: 558 us -> 0 us
  Pallas kernels: 0 us -> 173 us
  matrix products: 106 us -> 0 us
  blocking collectives: 86.7 us -> 0 us
  local copies, waits for them, and re-layouts: 36.4 us -> 6.95 us
  other arithmetic: 30.4 us -> 12.2 us
  between operations: 15.2 us -> 0.99 us
    all_gather x6 -> x0, waiting for transfers between devices: 251 us -> none  [the longest x4 240 us: gather_whole(): return lax.all_gather(part, 'tensor', axis=tensor_dim, tiled=True)]
    reduce_scatter x5 -> x0, waiting for transfers between devices: 190 us -> none  [the longest x3 115 us: scatter_sum(): lax.psum_scatter(whole.astype(jnp.bfloat16), 'tensor', scatter_dimension=...]
    pallas_call x0 -> x1, Pallas kernels: none -> 173 us  [run_layer(): pl.pallas_call(layer_kernel, name='encoder_layer', out_shape=(jax.ShapeDt...]
    unnamed x17 -> x0, waiting for transfers between devices: 116 us -> none
    dot_general x24 -> x0, matrix products: 106 us -> none  [the longest x1 19.6 us: on_device(): jnp.dot(normed_low, up_full, preferred_element_type=jnp.float32) + up_bias]
    psum x1 -> x0, blocking collectives: 48 us -> none  [on_device(): inner_sum, vector_sum = lax.psum((inner_local, vector_local), axes)]
    all_gather x3 -> x0, blocking collectives: 38.7 us -> none  [the longest x2 25.6 us: gather_whole(): part = lax.all_gather(low_shard, 'dp', axis=dp_dim, tiled=True)]
    unnamed x117 -> x54, local copies, waits for them, and re-layouts: 29 us -> 4.62 us
  transfers between devices with their start and end apart: 14 -> 0, of which waited for: 12 -> 0; matrix products, arithmetic and copies ran while one was open for 16% -> 0% of each run, Pallas kernels for 0% -> 0%
where the time goes in v2:
time: 193 us
  Pallas kernels  173 us (90%)
  other arithmetic  12.2 us (6%)
  local copies, waits for them, and re-layouts  6.95 us (4%)
    pallas_call x1, Pallas kernels, run_layer(): pl.pallas_call(layer_kernel, name='encoder_layer', out_shape=(jax.ShapeDt...  173 us
    sub x6, other arithmetic, adam_update(): weight - step_rate * (step_ratio + weight_decay * weight)  7.57 us
    unnamed x54, local copies, waits for them, and re-layouts  4.62 us

profile of v2, /device:TPU:0, one launch (start us, length us, event | category | flops | bytes accessed | tf_op | source)
XLA Modules:
  0.0 193.0 jit_solution(13505588509368397606)
XLA Ops:
  0.7 1.0 convert_bitcast_fusion
  1.7 1.0 convert_bitcast_fusion.1
  2.7 1.0 convert.5
  3.7 0.1 copy.75
  3.8 0.1 maximum_bitcast_fusion
  3.9 0.8 pad_maximum_fusion.pack_ref
  4.8 0.1 copy.76
  4.9 0.1 reshape.46
  5.1 0.6 pad_maximum_fusion.2.bias_ref
  5.7 0.6 concatenate.22.vec_ref
  6.4 172.8 %encoder_layer.1 = (bf16[512,768]{1,0:T(8,128)(2,1)}, f32[512,768]{1,0:T(8,128)}, f32[3,96,768]{2,1,0:T(8,128)}, f32[16,768]{1,0:T(8,128)}) custom-call(bf16[2048,768]{1,0:T(8,128)(2,1)} %tokens_hbm.1, bf16[512,768]{1,0:T(8,128)(2,1)} %cot_ref.1, s32[4,512]{1,0:T(4,128)} %seg_ref.1, bf16[3,96,768]{2,1,0:T(8,128)(2,1)} %pad_maximum_fusion.pack_ref, ...), custom_call_target="tpu_custom_call" | custom-call | tf_op jit(solution)/shard_map/encoder_layer/pallas_call | solution.py:873
  179.2 1.2 fusion.12
  180.5 1.1 multiply_subtract_fusion.2
  181.8 1.1 multiply_subtract_fusion.3
  182.8 0.7 copy.82
  183.6 0.7 copy.83
  184.3 0.7 copy.84
  185.0 2.0 %multiply_subtract_fusion.1 = (f32[96,768]{1,0:T(8,128)}, f32[96,768]{1,0:T(8,128)}, f32[96,768]{1,0:T(8,128)}) fusion(f32[96,768]{1,0:T(8,128)S(1)} %copy-done.2, f32[3,96,768]{2,1,0:T(8,128)} %get-tuple-element.26, f32[96,768]{1,0:T(8,128)S(1)} %copy-done.7, f32[96,768]{1,0:T(8,128)S(1)} %copy-done.8), kind=kLoop, calls=%fused_computation.12 | loop fusion | flops 1032192 | bytes 2064384 | tf_op jit(solution)/shard_map/sub | solution.py:40
  187.2 2.2 %multiply_subtract_fusion = (f32[768,96]{0,1:T(8,128)}, f32[768,96]{0,1:T(8,128)}, f32[768,96]{0,1:T(8,128)}) fusion(f32[768,96]{0,1:T(8,128)S(1)} %copy-done.3, f32[3,96,768]{2,1,0:T(8,128)} %get-tuple-element.26, f32[768,96]{0,1:T(8,128)S(1)} %copy-done.9, f32[768,96]{0,1:T(8,128)S(1)} %copy-done.10), kind=kLoop, calls=%fused_computation.11 | loop fusion | flops 1032192 | bytes 2064384 | tf_op jit(solution)/shard_map/sub | solution.py:40
  189.4 0.1 reshape_squeeze.3
  189.7 0.6 multiply_subtract_fusion.5
  190.3 0.6 multiply_subtract_fusion.4
  190.9 0.9 copy.87
  191.8 1.1 copy.88
  (59 shorter events, 0.6 us)
Async XLA Ops:
  0.7 3.0 %copy-start.11 = (f32[192,96]{1,0:T(8,128)S(1)}, f32[192,96]{1,0:T(8,128)}, u32[]{:S(2)}) copy-start(f32[192,96]{1,0:T(8,128)} %param.27) | copy-start | bytes 221188
  0.7 4.1 %copy-start.16 = (f32[6,192]{1,0:T(8,128)S(1)}, f32[6,192]{1,0:T(8,128)}, u32[]{:S(2)}) copy-start(f32[6,192]{1,0:T(8,128)} %param.36) | copy-start | bytes 13828
  1.7 4.0 %copy-start.14 = (f32[6,768]{1,0:T(8,128)S(1)}, f32[6,768]{1,0:T(8,128)}, u32[]{:S(2)}) copy-start(f32[6,768]{1,0:T(8,128)} %param.39) | copy-start | bytes 55300
  6.4 174.0 %copy-start.1 = (f32[3,96,192]{2,1,0:T(8,128)S(1)}, f32[3,96,192]{2,1,0:T(8,128)}, u32[]{:S(2)}) copy-start(f32[3,96,192]{2,1,0:T(8,128)} %param.24) | copy-start | bytes 663556
  6.4 174.1 %copy-start.5 = (f32[3,96,192]{2,1,0:T(8,128)S(1)}, f32[3,96,192]{2,1,0:T(8,128)}, u32[]{:S(2)}) copy-start(f32[3,96,192]{2,1,0:T(8,128)} %param.25) | copy-start | bytes 663556
  6.4 174.1 %copy-start.6 = (f32[3,96,192]{2,1,0:T(8,128)S(1)}, f32[3,96,192]{2,1,0:T(8,128)}, u32[]{:S(2)}) copy-start(f32[3,96,192]{2,1,0:T(8,128)} %param.26) | copy-start | bytes 663556
  179.2 2.3 %copy-start.12 = (f32[192,96]{1,0:T(8,128)S(1)}, f32[192,96]{1,0:T(8,128)}, u32[]{:S(2)}) copy-start(f32[192,96]{1,0:T(8,128)} %param.28) | copy-start | bytes 221188
  179.2 2.4 %copy-start.13 = (f32[192,96]{1,0:T(8,128)S(1)}, f32[192,96]{1,0:T(8,128)}, u32[]{:S(2)}) copy-start(f32[192,96]{1,0:T(8,128)} %param.29) | copy-start | bytes 221188
  180.4 4.6 %copy-start.2 = (f32[96,768]{1,0:T(8,128)S(1)}, f32[96,768]{1,0:T(8,128)}, u32[]{:S(2)}) copy-start(f32[96,768]{1,0:T(8,128)} %param.30) | copy-start | bytes 884740
  180.4 4.6 %copy-start.7 = (f32[96,768]{1,0:T(8,128)S(1)}, f32[96,768]{1,0:T(8,128)}, u32[]{:S(2)}) copy-start(f32[96,768]{1,0:T(8,128)} %param.31) | copy-start | bytes 884740
  180.4 4.6 %copy-start.8 = (f32[96,768]{1,0:T(8,128)S(1)}, f32[96,768]{1,0:T(8,128)}, u32[]{:S(2)}) copy-start(f32[96,768]{1,0:T(8,128)} %param.32) | copy-start | bytes 884740
  181.7 5.4 %copy-start.3 = (f32[768,96]{0,1:T(8,128)S(1)}, f32[768,96]{0,1:T(8,128)}, u32[]{:S(2)}) copy-start(f32[768,96]{0,1:T(8,128)} %param.33) | copy-start | bytes 884740
  181.7 5.4 %copy-start.9 = (f32[768,96]{0,1:T(8,128)S(1)}, f32[768,96]{0,1:T(8,128)}, u32[]{:S(2)}) copy-start(f32[768,96]{0,1:T(8,128)} %param.34) | copy-start | bytes 884740
  181.7 5.4 %copy-start.10 = (f32[768,96]{0,1:T(8,128)S(1)}, f32[768,96]{0,1:T(8,128)}, u32[]{:S(2)}) copy-start(f32[768,96]{0,1:T(8,128)} %param.35) | copy-start | bytes 884740
  185.0 4.3 %copy-start.20 = (f32[16,768]{1,0:T(8,128)S(1)}, f32[16,768]{1,0:T(8,128)}, u32[]{:S(2)}) copy-start(f32[16,768]{1,0:T(8,128)} %get-tuple-element.27) | copy-start | bytes 147460
  187.1 2.6 %copy-start.17 = (f32[6,192]{1,0:T(8,128)S(1)}, f32[6,192]{1,0:T(8,128)}, u32[]{:S(2)}) copy-start(f32[6,192]{1,0:T(8,128)} %param.36) | copy-start | bytes 13828
  187.1 2.6 %copy-start.21 = (f32[6,192]{1,0:T(8,128)S(1)}, f32[6,192]{1,0:T(8,128)}, u32[]{:S(2)}) copy-start(f32[6,192]{1,0:T(8,128)} %param.37) | copy-start | bytes 13828
  187.1 2.6 %copy-start.22 = (f32[6,192]{1,0:T(8,128)S(1)}, f32[6,192]{1,0:T(8,128)}, u32[]{:S(2)}) copy-start(f32[6,192]{1,0:T(8,128)} %param.38) | copy-start | bytes 13828
  187.1 3.2 %copy-start.15 = (f32[6,768]{1,0:T(8,128)S(1)}, f32[6,768]{1,0:T(8,128)}, u32[]{:S(2)}) copy-start(f32[6,768]{1,0:T(8,128)} %param.39) | copy-start | bytes 55300
  187.1 3.2 %copy-start.18 = (f32[6,768]{1,0:T(8,128)S(1)}, f32[6,768]{1,0:T(8,128)}, u32[]{:S(2)}) copy-start(f32[6,768]{1,0:T(8,128)} %param.40) | copy-start | bytes 55300
  187.1 3.2 %copy-start.19 = (f32[6,768]{1,0:T(8,128)S(1)}, f32[6,768]{1,0:T(8,128)}, u32[]{:S(2)}) copy-start(f32[6,768]{1,0:T(8,128)} %param.41) | copy-start | bytes 55300
  187.1 3.8 %copy-start.4 = (bf16[512,768]{1,0:T(8,128)(2,1)S(1)}, bf16[512,768]{1,0:T(8,128)(2,1)}, u32[]{:S(2)}) copy-start(bf16[512,768]{1,0:T(8,128)(2,1)} %get-tuple-element.136) | copy-start | bytes 2359300
  187.2 4.7 %copy-start = (f32[512,768]{1,0:T(8,128)S(1)}, f32[512,768]{1,0:T(8,128)}, u32[]{:S(2)}) copy-start(f32[512,768]{1,0:T(8,128)} %get-tuple-element.137) | copy-start | bytes 4718596

commit v3 on v2

--- a/solution.py
+++ b/solution.py
@@ -306,8 +306,9 @@
 PLANES = 4
 CHIPS = 4
 TILE = 256
-SLOTS_HELD = 5
-LENT = 4
+KEPT = 8
+LEAVING = 2
+LENT = 2
 
 
 def mm(left, right):
@@ -335,30 +336,32 @@
 
 
 def layer_kernel(
-    tokens_hbm, cot_ref, seg_ref, pack_ref, bias_ref, vec_ref,
-    block_ref, tgrad_ref, grad_ref, small_ref,
-    W, TOK, XT, XT2, QKV, ATT, PT, PRE, RSTD, NB, PO, HID, GP, GB, DHP,
-    BIAS, MASK, G, SR, DR, PR, ZR, SMK, SMS, SMR, SMZ,
+    tokens_hbm, cot_hbm, seg_ref, inner_ref, vec_ref,
+    iw_in, im_in, iv_in, ow_in, om_in, ov_in, uw_in, um_in, uv_in, dw_in, dm_in, dv_in,
+    block_hbm, tgrad_hbm,
+    iw_out, im_out, iv_out, ow_out, om_out, ov_out, uw_out, um_out, uv_out, dw_out, dm_out, dv_out,
+    small_ref,
+    W, TOK, COT, XT, XT2, QKV, ATT, PT, PRE, RSTD, NB, PO, HID, GP, GB, DHP,
+    BIAS, MASK, OUT, OWN, SR, DR, PR, ZR, PZ, GRAD, SMK, SMS, SMR, SMZ,
+    IW, IM, IV, OW, OM, OV, UW, DW,
     gather_send, gather_recv, red_send, red_recv, small_send, small_recv, bias_send, bias_recv,
-    local_sem, credit_sem,
+    load_sem, store_sem, credit_sem,
 ):
     dp = lax.axis_index("dp")
     z = lax.axis_index("tensor")
-    core = dp % 2
-    chip = dp // 2
-    jx = (chip // 2) * 2 + (1 - chip % 2)
-    jy = (1 - chip // 2) * 2 + chip % 2
-    jd = 3 - chip
+    core = dp & 1
+    chip = dp >> 1
+    jx, jy, jd = chip ^ 1, chip ^ 2, chip ^ 3
     n_tok = TOK.shape[0]
     width = TOK.shape[1]
-    rows = pack_ref.shape[1]
+    rows = IW.shape[1]
     half = rows // 2
     dev_sib = (chip * 2 + (1 - core), z)
     dev_x = (jx * 2 + core, z)
     dev_y = (jy * 2 + core, z)
 
     def plane(k):
-        return (z + k) % PLANES
+        return (z + k) & (PLANES - 1)
 
     def dev_z(k):
         return (dp, plane(k))
@@ -371,17 +374,42 @@
             src_ref=src, dst_ref=dst, send_sem=ssem, recv_sem=rsem, device_id=dev, device_id_type=MESH
         )
 
-    tok_copy = pltpu.make_async_copy(
-        tokens_hbm.at[pl.ds(pl.multiple_of(z * n_tok, 16), n_tok)], TOK, local_sem
-    )
-    tok_copy.start()
-    for m in range(3):
-        W[m, z, rd(chip, core), :] = pack_ref[m]
-    BIAS[z] = bias_ref[...]
-
     barrier = pltpu.get_barrier_semaphore()
     for dev in (dev_sib, dev_x, dev_y, dev_z(1), dev_z(2), dev_z(3)):
         pl.semaphore_signal(barrier, inc=1, device_id=dev, device_id_type=MESH)
+
+    UM, UV, DM, DV = (PO.at[pl.ds(i * rows, rows)] for i in range(4))
+    held_here = (IW, OW, UW, DW, IM, IV, OM, OV, UM, UV, DM, DV)
+    arrays_in = (iw_in, ow_in, uw_in, dw_in, im_in, iv_in, om_in, ov_in, um_in, uv_in, dm_in, dv_in)
+    arrays_out = (
+        iw_out, ow_out, uw_out, dw_out, im_out, iv_out, om_out, ov_out, um_out, uv_out, dm_out, dv_out
+    )
+    loads = [
+        pltpu.make_async_copy(src, dst, load_sem.at[i])
+        for i, (src, dst) in enumerate(zip(arrays_in, held_here))
+    ]
+    tok_copy = pltpu.make_async_copy(
+        tokens_hbm.at[pl.ds(pl.multiple_of(z * n_tok, 16), n_tok)], TOK, load_sem.at[12]
+    )
+    cot_copy = pltpu.make_async_copy(cot_hbm, COT, load_sem.at[13])
+    stores = [
+        pltpu.make_async_copy(src, dst, store_sem.at[i])
+        for i, (src, dst) in enumerate(zip(held_here, arrays_out))
+    ]
+    block_store = pltpu.make_async_copy(COT, block_hbm, store_sem.at[12])
+    tgrad_store = pltpu.make_async_copy(PRE, tgrad_hbm, store_sem.at[13])
+    for copy in loads[:4] + [tok_copy, cot_copy] + loads[4:8]:
+        copy.start()
+    local = 3 * DH
+    loads[0].wait()
+    loads[1].wait()
+    W[0, z, rd(chip, core), :] = jnp.concatenate(
+        [IW[0], IW[1], OW[...].T, IW[2]], axis=1
+    ).astype(BF16)
+    loads[2].wait()
+    W[1, z, rd(chip, core), :] = UW[...].astype(BF16)
+    loads[3].wait()
+    W[2, z, rd(chip, core), :] = DW[...].astype(BF16)
     pl.semaphore_wait(barrier, 6)
 
     def send_block(m, t, j, c, kind, dev, start=0, size=rows):
@@ -389,13 +417,33 @@
         return remote(region, region, gather_send.at[m, kind], gather_recv.at[m, kind], dev)
 
     def wait_block(m, t, j, c, kind, start=0, size=rows):
-        region = W.at[m, t, rd(j, c, start, size)]
+        region = W.at[0, 0, pl.ds(0, size)]
         remote(region, region, gather_send.at[m, kind], gather_recv.at[m, kind], dev_sib).wait_recv()
 
     def z_sends(m):
         for k in (1, 2, 3):
             send_block(m, z, chip, core, k - 1, dev_z(PLANES - k)).start()
 
+    def handed(m, at, k):
+        near = ((k == 1) & (at < PLANES - 1)) | ((k == 3) & (at > 0))
+        edge = (at == 0) | (at == PLANES - 1)
+        return near & ((m == 2) | ((m == 1) & edge))
+
+    def pass_on(m, j, which, act):
+        @pl.when((z < PLANES - 1) & handed(m, z + 1, 3))
+        def _():
+            act(send_block(m, z, j, core, 38 + which, dev_z(1)))
+
+        @pl.when((z > 0) & handed(m, z - 1, 1))
+        def _():
+            act(send_block(m, z, j, core, 35 + which, dev_z(3)))
+
+    def start(copy):
+        copy.start()
+
+    def sent(copy):
+        copy.wait_send()
+
     def first(m, k):
         t = plane(k)
 
@@ -403,56 +451,121 @@
         def _():
             wait_block(m, t, chip, core, k - 1)
 
-        send_block(m, t, chip, core, 3 + k, dev_x).start()
-        send_block(m, t, chip, core, 7 + k, dev_y).start()
+        @pl.when(jnp.logical_not(handed(m, z, k)))
+        def _():
+            send_block(m, t, chip, core, 3 + k, dev_x).start()
+            send_block(m, t, chip, core, 7 + k, dev_y).start()
+
         send_block(m, t, chip, core, 19 + k, dev_sib).start()
 
     def second(m, k):
         t = plane(k)
-        wait_block(m, t, jx, core, 3 + k)
-        send_block(m, t, jx, core, 15 + k, dev_y, 0, half).start()
-        wait_block(m, t, jy, core, 7 + k)
-        send_block(m, t, jy, core, 11 + k, dev_x, half, half).start()
+        away = handed(m, z, k)
+
+        @pl.when(away)
+        def _():
+            wait_block(m, t, jx, core, 35 + 3 * (k >> 1))
+            wait_block(m, t, jy, core, 36 + 3 * (k >> 1))
+
+        @pl.when(jnp.logical_not(away))
+        def _():
+            wait_block(m, t, jx, core, 3 + k)
+            send_block(m, t, jx, core, 15 + k, dev_y, 0, half).start()
+            wait_block(m, t, jy, core, 7 + k)
+            send_block(m, t, jy, core, 11 + k, dev_x, half, half).start()
+
         send_block(m, t, jx, core, 23 + k, dev_sib).start()
         send_block(m, t, jy, core, 27 + k, dev_sib).start()
 
+        @pl.when(k == 0)
+        def _():
+            pass_on(m, jx, 0, start)
+            pass_on(m, jy, 1, start)
+
     def third(m, k):
         t = plane(k)
-        wait_block(m, t, jd, core, 15 + k, 0, half)
-        wait_block(m, t, jd, core, 11 + k, half, half)
+        away = handed(m, z, k)
+
+        @pl.when(away)
+        def _():
+            wait_block(m, t, jd, core, 37 + 3 * (k >> 1))
+
+        @pl.when(jnp.logical_not(away))
+        def _():
+            wait_block(m, t, jd, core, 15 + k, 0, half)
+            wait_block(m, t, jd, core, 11 + k, half, half)
+
         send_block(m, t, jd, core, 31 + k, dev_sib).start()
+
+        @pl.when(k == 0)
+        def _():
+            pass_on(m, jd, 2, start)
+
+    def fourth(m, k):
+        t = plane(k)
         wait_block(m, t, chip, 1 - core, 19 + k)
         wait_block(m, t, jx, 1 - core, 23 + k)
         wait_block(m, t, jy, 1 - core, 27 + k)
         wait_block(m, t, jd, 1 - core, 31 + k)
 
-    def gather_step(i):
-        @pl.when(i < 10)
-        def _():
-            nxt = i + 2
-            m, k = nxt // PLANES, nxt % PLANES
-            first(m, k)
-
-            @pl.when((k == 1) & (m < 2))
+    def third_of(i):
+        return (i * 11) >> 5
+
+    def place(i):
+        later = (i >= 3).astype(jnp.int32) if not isinstance(i, int) else int(i >= 3)
+        m = i - later * (i - third_of(i - 3))
+        return m, later * (i - 2 - 3 * m)
+
+    def gather_calls(i):
+        def start_next():
+            @pl.when(i < 9)
             def _():
-                z_sends(m + 1)
-
-        @pl.when(i < 11)
-        def _():
-            nxt = i + 1
-            second(nxt // PLANES, nxt % PLANES)
-
-        third(i // PLANES, i % PLANES)
-
-    z_sends(0)
+                first(*place(i + 3))
+
+        def middle():
+            @pl.when(i < 11)
+            def _():
+                second(*place(i + 1))
+
+        def last():
+            @pl.when((i > 0) & (i <= 12))
+            def _():
+                third(*place(i - 1))
+
+        def whole():
+            @pl.when((i > 1) & (i <= 13))
+            def _():
+                fourth(*place(i - 2))
+
+        return start_next, middle, last, whole
+
+    first(0, 0)
+    first(1, 0)
+    first(2, 0)
+    spread = lax.broadcasted_iota(jnp.int32, (local, width), 1) - PLANES * lax.broadcasted_iota(
+        jnp.int32, (local, width), 0
+    )
+    up_row = jnp.zeros((1, width), F32)
+    for r in range(4):
+        up_row += lax.dot_general(
+            inner_ref[2 + r : 3 + r, :],
+            jnp.where(spread == r, 1.0, 0.0),
+            (((1,), (0,)), ((), ())),
+            precision=lax.Precision.HIGHEST,
+            preferred_element_type=F32,
+        )
+    BIAS[z, 0:1, :] = jnp.concatenate(
+        [inner_ref[0:1, :], jnp.zeros((1, 2 * local), F32), inner_ref[1:2, :]], axis=1
+    )
+    BIAS[z, 1:2, :] = up_row
     for k in (1, 2, 3):
         remote(
             BIAS.at[z], BIAS.at[z], bias_send.at[k - 1], bias_recv.at[k - 1], dev_z(PLANES - k)
         ).start()
-    first(0, 0)
+    z_sends(0)
+    z_sends(1)
+    z_sends(2)
     tok_copy.wait()
-    first(0, 1)
-    z_sends(1)
     second(0, 0)
 
     vec = vec_ref[...]
@@ -478,7 +591,18 @@
     lane = lax.broadcasted_iota(jnp.int32, (1, width), 1)
     q_scale = jnp.where(lane < 3 * DH, 1.0 / math.sqrt(DH), 1.0)
     heads = 3
-    local = heads * DH
+    for i in range(3):
+        for call in gather_calls(i):
+            call()
+
+    def early(k, i):
+        def call():
+            @pl.when(k == 0)
+            def _():
+                for part in gather_calls(i):
+                    part()
+
+        return call
 
     def forward_attention(k):
         t = plane(k)
@@ -486,6 +610,7 @@
             cols = slice(n * TILE, (n + 1) * TILE)
             res = mm(TOK[...], W[0, t, :, cols]) + BIAS[t, 0:1, cols]
             QKV[k, :, cols] = (res * q_scale[:, cols]).astype(BF16)
+        yield
         attended = []
         for h in range(heads):
             query = QKV[k, :, h * DH : (h + 1) * DH]
@@ -502,6 +627,7 @@
                 PT[k, h, b] = soft
                 outs.append(mm_tn(soft, values[128 * b : 128 * b + span]))
             attended.append(jnp.concatenate(outs, axis=0))
+            yield
         out = jnp.concatenate(attended, axis=1).astype(BF16)
         ATT[k] = out
         for n in range(3):
@@ -530,22 +656,36 @@
             cdf, slope = gelu_parts(u)
             HID[k, :, cols] = (u * cdf).astype(BF16)
             GP[k, :, cols] = slope.astype(BF16)
+            yield
 
     def forward_down(k):
         t = plane(k)
         for n in range(3):
             cols = slice(n * TILE, (n + 1) * TILE)
             PO[:, cols] += mm_nt(HID[k], W[2, t, cols, :])
+            yield
+
+    def weave(work, calls):
+        calls = list(calls)
+        for _ in work:
+            if calls:
+                calls.pop(0)()
+        for call in calls:
+            call()
 
     for p, work in enumerate((forward_attention, forward_up, forward_down)):
 
         @pl.loop(0, PLANES)
         def _(k, p=p, work=work):
-            gather_step(p * PLANES + k)
-            work(k)
+            calls = gather_calls(jnp.where(k < 3, 3 * p + k + 5, 99))
+            if p == 0:
+                calls = tuple(early(k, i) for i in (3, 4)) + calls
+            weave(work(k), calls)
 
         if p == 0:
             forward_norm()
+
+    cot_copy.wait()
 
     SMK[...] = jnp.zeros_like(SMK)
     SMS[...] = jnp.zeros_like(SMS)
@@ -557,8 +697,8 @@
         centered = rows_in - jnp.mean(rows_in, axis=-1, keepdims=True)
         scale = lax.rsqrt(jnp.mean(centered * centered, axis=-1, keepdims=True) + NORM_EPS)
         unit = centered * scale
-        block_ref[part, :] = (unit * vec[4:5] + vec[5:6]).astype(BF16)
-        cot = cot_ref[part, :].astype(F32)
+        cot = COT[part, :].astype(F32)
+        COT[part, :] = (unit * vec[4:5] + vec[5:6]).astype(BF16)
         e = cot * vec[4:5]
         grad = scale * (
             e
@@ -571,33 +711,57 @@
         SMS[12:13, :] += jnp.sum(cot * unit, axis=0, keepdims=True)
         SMS[13:14, :] += jnp.sum(cot, axis=0, keepdims=True)
 
+    block_store.start()
+
     def unit_rows(j, start=0, size=rows):
         return pl.ds(pl.multiple_of(j * rows + start, 16), size)
 
-    def red(src, dst, u, stage, dev):
+    def red(src, dst, p, kk, stage, dev):
+        u = PLANES * p + kk
         return remote(src, dst, red_send.at[u, stage], red_recv.at[u, stage], dev)
 
-    def held(u, j, start=0, size=rows):
-        return G.at[u % SLOTS_HELD, core, unit_rows(j, start, size)]
+    def spot(p, kk):
+        n = 3 * p + kk
+        return jnp.where(kk == PLANES - 1, KEPT + p, n - jnp.where(n >= KEPT, KEPT, 0))
+
+    def kept(p, kk, j, start=0, size=rows):
+        return OWN.at[spot(p, kk), unit_rows(j, start, size)]
+
+    def add_to(p, kk, j, others, start=0, size=rows):
+        at, here = spot(p, kk), unit_rows(j, start, size)
+        total = OWN[at, here, :].astype(F32)
+        for other in others:
+            total = total + other.astype(F32)
+        return at, here, total
+
+    def handed_back(p, kk):
+        return handed(2 - p, z, kk + 1)
 
     def to_sibling(u):
-        return red(G.at[u % SLOTS_HELD, 1 - core], SR.at[u % LENT], u, 0, dev_sib)
-
-    def relay_y(u):
-        return red(held(u, jd, 0, half), DR.at[u, 0], u, 1, dev_y)
-
-    def relay_x(u):
-        return red(held(u, jd, half, half), DR.at[u, 1], u, 2, dev_x)
-
-    def along_x(u):
-        return red(held(u, jx), PR.at[u, 0], u, 3, dev_x)
-
-    def along_y(u):
-        return red(held(u, jy), PR.at[u, 1], u, 4, dev_y)
-
-    def along_z(u):
-        kk = u % PLANES
-        return red(held(u, chip), ZR.at[u // PLANES, kk], u, 5, (dp, (z + 1 + kk) % PLANES))
+        return red(
+            OUT.at[u & (LEAVING - 1)], SR.at[u & (LENT - 1)], u >> 2, u & 3, 0, dev_sib
+        )
+
+    def relay_y(p, kk):
+        return red(kept(p, kk, jd, 0, half), DR.at[4 * p + kk, 0], p, kk, 1, dev_y)
+
+    def relay_x(p, kk):
+        return red(kept(p, kk, jd, half, half), DR.at[4 * p + kk, 1], p, kk, 2, dev_x)
+
+    def along_x(p, kk):
+        return red(kept(p, kk, jx), PR.at[4 * p + kk, 0], p, kk, 3, dev_x)
+
+    def along_y(p, kk):
+        return red(kept(p, kk, jy), PR.at[4 * p + kk, 1], p, kk, 4, dev_y)
+
+    def along_z(p, kk):
+        return red(kept(p, kk, chip), ZR.at[p, kk], p, kk, 5, (dp, (z + 1 + kk) & (PLANES - 1)))
+
+    def all_along_z(p, kk):
+        side = jnp.where(p == 0, kk >> 1, 2)
+        return red(
+            OWN.at[spot(p, kk)], PZ.at[side], p, kk, 5, (dp, (z + 1 + kk) & (PLANES - 1))
+        )
 
     def step_one(u):
         @pl.when(u >= LENT)
@@ -608,89 +772,136 @@
 
     def step_two(u):
         to_sibling(u).wait_recv()
-
-        def merge(j):
-            here = unit_rows(j)
-            slot = u % SLOTS_HELD
-            both = G[slot, core, here, :].astype(F32) + SR[u % LENT, here, :].astype(F32)
-            G[slot, core, here, :] = both.astype(BF16)
-
-        merge(jd)
-        relay_y(u).start()
-        relay_x(u).start()
-        merge(jx)
-        merge(jy)
-        merge(chip)
+        p, kk = u >> 2, u & 3
+        for j in range(CHIPS):
+            at, here, total = add_to(p, kk, j, [SR[u & (LENT - 1), unit_rows(j), :]])
+            OWN[at, here, :] = total.astype(BF16)
 
         @pl.when(u < 12 - LENT)
         def _():
             pl.semaphore_signal(credit_sem, inc=1, device_id=dev_sib, device_id_type=MESH)
 
-    def step_three(u):
-        slot = u % SLOTS_HELD
-        relay_y(u).wait_recv()
-        here = unit_rows(jx, 0, half)
-        G[slot, core, here, :] = (
-            G[slot, core, here, :].astype(F32) + DR[u, 0].astype(F32)
-        ).astype(BF16)
-        along_x(u).start()
-        relay_x(u).wait_recv()
-        here = unit_rows(jy, half, half)
-        G[slot, core, here, :] = (
-            G[slot, core, here, :].astype(F32) + DR[u, 1].astype(F32)
-        ).astype(BF16)
-        along_y(u).start()
-
-    def step_four(u):
-        slot = u % SLOTS_HELD
-        along_x(u).wait_recv()
-        along_y(u).wait_recv()
-        here = unit_rows(chip)
-        own = (
-            G[slot, core, here, :].astype(F32) + PR[u, 0].astype(F32) + PR[u, 1].astype(F32)
-        )
-
-        @pl.when(u % PLANES < PLANES - 1)
-        def _():
-            G[slot, core, here, :] = own.astype(BF16)
-            along_z(u).start()
-
-        @pl.when(u % PLANES == PLANES - 1)
-        def _():
-            grad_ref[u // PLANES] = own
-
-    def sends_done(u):
-        to_sibling(u).wait_send()
-        relay_y(u).wait_send()
-        relay_x(u).wait_send()
-        along_x(u).wait_send()
-        along_y(u).wait_send()
-
-        @pl.when(u % PLANES < PLANES - 1)
-        def _():
-            along_z(u).wait_send()
+    def take_handed(p, kk, from_below):
+        at_k = 1 if from_below else 3
+        at_z = z - 1 if from_below else z + 1
+        there = (at_z >= 0) & (at_z < PLANES)
+
+        @pl.when((kk == PLANES - 1) & there & handed(2 - p, at_z, at_k))
+        def _():
+            side = jnp.where(p == 0, (at_k - 1) // 2, 2)
+            red(PZ.at[0], PZ.at[0], p, at_k - 1, 5, dev_sib).wait_recv()
+            for j in range(CHIPS):
+                at, here, total = add_to(p, kk, j, [PZ[side, unit_rows(j), :]])
+                OWN[at, here, :] = total.astype(BF16)
+
+    def step_three(p, kk):
+        take_handed(p, kk, True)
+        take_handed(p, kk, False)
+        away = handed_back(p, kk)
+
+        @pl.when(away)
+        def _():
+            all_along_z(p, kk).start()
+
+        @pl.when(jnp.logical_not(away))
+        def _():
+            relay_y(p, kk).start()
+            relay_x(p, kk).start()
+
+    def step_four(p, kk):
+        @pl.when(jnp.logical_not(handed_back(p, kk)))
+        def _():
+            u = 4 * p + kk
+            relay_y(p, kk).wait_recv()
+            at, here, total = add_to(p, kk, jx, [DR[u, 0]], 0, half)
+            OWN[at, here, :] = total.astype(BF16)
+            along_x(p, kk).start()
+            relay_x(p, kk).wait_recv()
+            at, here, total = add_to(p, kk, jy, [DR[u, 1]], half, half)
+            OWN[at, here, :] = total.astype(BF16)
+            along_y(p, kk).start()
+
+    def step_five(p, kk):
+        @pl.when(jnp.logical_not(handed_back(p, kk)))
+        def _():
+            u = 4 * p + kk
+            along_x(p, kk).wait_recv()
+            along_y(p, kk).wait_recv()
+            at, here, total = add_to(p, kk, chip, [PR[u, 0], PR[u, 1]])
+
+            @pl.when(kk < PLANES - 1)
+            def _():
+                OWN[at, here, :] = total.astype(BF16)
+                along_z(p, kk).start()
+
+            @pl.when(kk == PLANES - 1)
+            def _():
+                GRAD[p] = total
+
+    def sends_done(p, kk):
+        away = handed_back(p, kk)
+
+        @pl.when(away)
+        def _():
+            all_along_z(p, kk).wait_send()
+
+        @pl.when(jnp.logical_not(away))
+        def _():
+            relay_y(p, kk).wait_send()
+            relay_x(p, kk).wait_send()
+            along_x(p, kk).wait_send()
+            along_y(p, kk).wait_send()
+
+            @pl.when(kk < PLANES - 1)
+            def _():
+                along_z(p, kk).wait_send()
+
+    def item(i):
+        p = third_of(i)
+        kk = i - 3 * p
+        late = (i == 6) | (i >= 10)
+        p = jnp.where(i == 6, 0, jnp.where(i == 10, 1, jnp.where(i > 6, 2, p)))
+        kk = jnp.where(late, PLANES - 1, jnp.where(i > 6, i - 7, kk))
+        return p, kk
+
+    def reduce_calls(u):
+        def merge():
+            @pl.when((u >= 1) & (u < 13))
+            def _():
+                step_two(u - 1)
+
+        def stage(lag, step):
+            i = u - lag
+            i = jnp.where(i >= 3, i - 1, i)
+
+            def call():
+                @pl.when((u >= lag) & (u != lag + 3) & (i < 12))
+                def _():
+                    step(*item(i))
+
+            return call
+
+        def merge_and_relay():
+            merge()
+            stage(1, step_three)()
+
+        return stage(3, step_four), stage(4, step_five), merge_and_relay
 
     def reduce_step(u):
-        @pl.when(u < 12)
-        def _():
-            step_one(u)
-
-        @pl.when((u >= 1) & (u < 13))
-        def _():
-            step_two(u - 1)
-
-        @pl.when((u >= 2) & (u < 14))
-        def _():
-            step_three(u - 2)
-
-        @pl.when((u >= 3) & (u < 15))
-        def _():
-            step_four(u - 3)
+        for call in reduce_calls(u):
+            call()
 
     def before_unit(u):
-        @pl.when(u >= SLOTS_HELD)
-        def _():
-            sends_done(u - SLOTS_HELD)
+        p, kk = u >> 2, u & 3
+        old = 3 * p + kk - KEPT
+
+        @pl.when((kk < PLANES - 1) & (old >= 0))
+        def _():
+            sends_done(third_of(old), old - 3 * third_of(old))
+
+        @pl.when(u >= LEAVING)
+        def _():
+            to_sibling(u - LEAVING).wait_send()
 
     def transposed(src, dst):
         for j in range(CHIPS):
@@ -699,29 +910,36 @@
                 dst[c, j * rows : (j + 1) * rows, :] = src[:, lo : lo + rows].T
 
     def fill(u, left, right_of, lo, hi):
-        slot = u % SLOTS_HELD
-        for c in range(2):
-            G[slot, c, :, lo:hi] = mm(left[c], right_of(lo, hi)).astype(BF16)
+        OUT[u & (LEAVING - 1), :, lo:hi] = mm(left[1 - core], right_of(lo, hi)).astype(BF16)
+        OWN[spot(u >> 2, u & 3), :, lo:hi] = mm(left[core], right_of(lo, hi)).astype(BF16)
 
     transposed(GB, XT)
 
     def backward_down(u, k):
+        yield
         for n in range(3):
             fill(u, XT, lambda lo, hi: HID[k, :, lo:hi], n * TILE, (n + 1) * TILE)
+            yield
+        step_one(u)
 
     def backward_up(u, k):
         t = plane(k)
+        yield
         for n in range(3):
             cols = slice(n * TILE, (n + 1) * TILE)
             grad = mm(GB[...], W[2, t, :, cols]) * GP[k, :, cols].astype(F32)
             low = grad.astype(BF16)
             DHP[:, cols] = low
             SMK[t, 1:2, cols] = jnp.sum(low.astype(F32), axis=0, keepdims=True)
+        yield
         for n in range(3):
             fill(u, XT, lambda lo, hi: DHP[:, lo:hi], n * TILE, (n + 1) * TILE)
+        step_one(u)
+        yield
         for n in range(3):
             cols = slice(n * TILE, (n + 1) * TILE)
             PO[:, cols] += mm_nt(DHP[...], W[1, t, cols, :])
+        yield
 
     def backward_norm():
         @pl.loop(0, 8)
@@ -735,7 +953,7 @@
                 - jnp.mean(e, axis=-1, keepdims=True)
                 - unit * jnp.mean(e * unit, axis=-1, keepdims=True)
             )
-            tgrad_ref[part, :] = grad
+            PRE[part, :] = grad
             GB[part, :] = grad.astype(BF16)
             SMS[8:9, :] += jnp.sum(grad, axis=0, keepdims=True)
             SMS[9:10, :] += jnp.sum(grad_in * unit, axis=0, keepdims=True)
@@ -743,6 +961,7 @@
 
     def backward_attention(u, k):
         t = plane(k)
+        yield
         back = mm(GB[...], W[0, t, :, 2 * local : 3 * local]).astype(BF16)
         grads = ([], [], [])
         for h in range(heads):
@@ -771,6 +990,7 @@
             grads[0].append(jnp.concatenate(d_query, axis=0) * (1.0 / math.sqrt(DH)))
             grads[1].append(overlap(d_keys))
             grads[2].append(overlap(d_values))
+            yield
         empty = jnp.zeros((n_tok, local), F32)
         DHP[...] = jnp.concatenate(
             grads[0] + grads[1] + [empty] + grads[2], axis=1
@@ -779,9 +999,51 @@
         fill(u, XT, lambda lo, hi: DHP[:, lo:hi], 0, 2 * local)
         fill(u, XT2, lambda lo, hi: ATT[k], 2 * local, 3 * local)
         fill(u, XT, lambda lo, hi: DHP[:, lo:hi], 3 * local, 4 * local)
+        step_one(u)
+        yield
         for n in range(3):
             cols = slice(n * TILE, (n + 1) * TILE)
-            tgrad_ref[:, cols] += mm_nt(DHP[...], W[0, t, cols, :])
+            PRE[:, cols] += mm_nt(DHP[...], W[0, t, cols, :])
+
+    def whole_gradient(p):
+        for kk in range(3):
+
+            @pl.when(jnp.logical_not(handed(2 - p, (z + 3 - kk) & (PLANES - 1), kk + 1)))
+            def _(kk=kk):
+                red(ZR.at[p, kk], ZR.at[p, kk], p, kk, 5, dev_sib).wait_recv()
+                GRAD[p] += ZR[p, kk].astype(F32)
+
+        return GRAD[p]
+
+    def update(arrays, gradient, rate, *index):
+        where = index if index else (Ellipsis,)
+        w, m, v = (ref[where] for ref in arrays)
+        for ref, new in zip(arrays, adam_update(w, m, v, gradient, rate, WEIGHT_DECAY)):
+            ref[where] = new
+
+    def finish(p):
+        if p == 0:
+            for i in (3, 10, 11):
+                if i > 3:
+                    loads[i].wait()
+            update((DW, DM, DV), whole_gradient(0), RATE_DOWN)
+            for i in (3, 10, 11):
+                stores[i].start()
+        if p == 1:
+            loads[8].wait()
+            loads[9].wait()
+            update((UW, UM, UV), whole_gradient(1), RATE_UP)
+            for i in (2, 8, 9):
+                stores[i].start()
+        if p == 2:
+            for i in (4, 5, 6, 7):
+                loads[i].wait()
+            total = whole_gradient(2)
+            update((OW, OM, OV), total[:, 2 * local : 3 * local].T, RATE_OUTPUT)
+            for i, at in enumerate((0, 1, 3)):
+                update((IW, IM, IV), total[:, at * local : (at + 1) * local], RATE_INPUT, i)
+            for i in (0, 1, 4, 5, 6, 7):
+                stores[i].start()
 
     for p, work in enumerate((backward_down, backward_up, backward_attention)):
 
@@ -789,15 +1051,20 @@
         def _(kk, p=p, work=work):
             u = p * PLANES + kk
             before_unit(u)
-            work(u, (kk + 1) % PLANES)
-            reduce_step(u)
+            weave(work(u, (kk + 1) & 3), reduce_calls(u))
 
         if p == 0:
             transposed(NB, XT)
         if p == 1:
             backward_norm()
+            for copy in loads[8:]:
+                copy.start()
             transposed(TOK, XT)
             transposed(GB, XT2)
+        if p == 2:
+            finish(0)
+
+    tgrad_store.start()
 
     for t in range(PLANES):
         SMS[2 * t : 2 * t + 2, :] = SMK[t, 0:2, :]
@@ -825,15 +1092,10 @@
         ).wait_recv()
     small_ref[...] = (SMZ[0] + SMZ[1]) + (SMZ[2] + SMZ[3])
 
-    for p in range(3):
-        total = grad_ref[p]
-        for kk in range(3):
-            remote(
-                ZR.at[p, kk], ZR.at[p, kk], red_send.at[4 * p + kk, 5],
-                red_recv.at[4 * p + kk, 5], dev_sib,
-            ).wait_recv()
-            total = total + ZR[p, kk].astype(F32)
-        grad_ref[p] = total
+    reduce_step(15)
+    finish(1)
+    reduce_step(16)
+    finish(2)
 
     for k in (1, 2, 3):
         small_z(k, dev_z(PLANES - k)).wait_send()
@@ -841,32 +1103,117 @@
             BIAS.at[z], BIAS.at[z], bias_send.at[k - 1], bias_recv.at[k - 1], dev_z(PLANES - k)
         ).wait_send()
 
-    @pl.loop(12 - SLOTS_HELD, 12)
+    @pl.loop(12 - LEAVING, 12)
     def _(u):
-        sends_done(u)
+        to_sibling(u).wait_send()
+
+    @pl.loop(9 - KEPT, 9)
+    def _(n):
+        sends_done(third_of(n), n - 3 * third_of(n))
 
     @pl.loop(0, 3)
-    def _(m):
-        for k in (1, 2, 3):
-            send_block(m, z, chip, core, k - 1, dev_z(PLANES - k)).wait_send()
-
-        @pl.loop(0, PLANES)
-        def _(k):
-            t = plane(k)
-            send_block(m, t, chip, core, 3 + k, dev_x).wait_send()
-            send_block(m, t, chip, core, 7 + k, dev_y).wait_send()
-            send_block(m, t, jx, core, 15 + k, dev_y, 0, half).wait_send()
-            send_block(m, t, jy, core, 11 + k, dev_x, half, half).wait_send()
+    def _(p):
+        sends_done(p, PLANES - 1)
+
+    def left(m, kind, size=rows):
+        region = W.at[0, 0, pl.ds(0, size)]
+        remote(region, region, gather_send.at[m, kind], gather_recv.at[m, kind], dev_sib).wait_send()
+
+    for m in range(3):
+        for kind in (0, 1, 2):
+            left(m, kind)
+        for which in range(3):
+            pass_on(m, chip, which, sent)
+        for k in range(PLANES):
+
+            @pl.when(jnp.logical_not(handed(m, z, k)))
+            def _(m=m, k=k):
+                left(m, 3 + k)
+                left(m, 7 + k)
+                left(m, 11 + k, half)
+                left(m, 15 + k, half)
+
             for kind in (19, 23, 27, 31):
-                send_block(m, t, chip, core, kind + k, dev_sib).wait_send()
-
-
-def run_layer(tokens, cotangent, segment_ids, packs, bias_rows, vectors):
+                left(m, kind + k)
+
+    for copy in stores + [block_store, tgrad_store]:
+        copy.wait()
+
+
+def hand_out_kernel(small_ref, iw, im, iv, vw, vm, vv, *refs):
+    moved = (len(refs) - 8) // 3
+    sources, targets = refs[:moved], refs[moved : 2 * moved]
+    iw_out, im_out, iv_out, vw_out, vm_out, vv_out = refs[2 * moved : 2 * moved + 6]
+    staged, sem = refs[2 * moved + 6 : -2], refs[-2:]
+    loads = [
+        pltpu.make_async_copy(src, mid, sem[0].at[i])
+        for i, (src, mid) in enumerate(zip(sources, staged))
+    ]
+    stores = [
+        pltpu.make_async_copy(mid, dst, sem[1].at[i])
+        for i, (mid, dst) in enumerate(zip(staged, targets))
+    ]
+    for copy in loads:
+        copy.start()
+    z = lax.axis_index("tensor")
+    small = small_ref[...]
+    width = small.shape[1]
+    local = iw.shape[1]
+    row_at = lax.broadcasted_iota(jnp.int32, small.shape, 0)
+    own = jnp.sum(jnp.where(row_at == 2 * z, small, 0.0), axis=0, keepdims=True)
+    own_up = jnp.sum(jnp.where(row_at == 2 * z + 1, small, 0.0), axis=0, keepdims=True)
+    spread = lax.broadcasted_iota(jnp.int32, (width, local), 0) - 4 * lax.broadcasted_iota(
+        jnp.int32, (width, local), 1
+    )
+    picked = [
+        lax.dot_general(
+            own_up,
+            jnp.where(spread == r, 1.0, 0.0),
+            (((1,), (0,)), ((), ())),
+            precision=lax.Precision.HIGHEST,
+            preferred_element_type=F32,
+        )
+        for r in range(4)
+    ]
+    for load, store in zip(loads, stores):
+        load.wait()
+        store.start()
+    inner_grad = jnp.concatenate([own[:, :local], own[:, 3 * local :], *picked], axis=0)
+    new = adam_update(iw[...], im[...], iv[...], inner_grad, RATE_VECTOR, 0.0)
+    iw_out[...], im_out[...], iv_out[...] = new
+    new = adam_update(vw[...], vm[...], vv[...], small[8:14], RATE_OUTER, 0.0)
+    vw_out[...], vm_out[...], vv_out[...] = new
+    for store in stores:
+        store.wait()
+
+
+def hand_out(small, *arrays):
+    params, moved = arrays[:6], arrays[6:]
+    vmem = pl.BlockSpec(memory_space=pltpu.VMEM)
+    hbm = pl.BlockSpec(memory_space=pl.ANY)
+    like = lambda v: jax.ShapeDtypeStruct(v.shape, v.dtype)
+    return pl.pallas_call(
+        hand_out_kernel,
+        name="hand_out",
+        out_shape=(*map(like, moved), *map(like, params)),
+        in_specs=[vmem] * 7 + [hbm] * len(moved),
+        out_specs=(hbm,) * len(moved) + (vmem,) * 6,
+        scratch_shapes=[
+            *(pltpu.VMEM(v.shape, v.dtype) for v in moved),
+            pltpu.SemaphoreType.DMA((len(moved),)),
+            pltpu.SemaphoreType.DMA((len(moved),)),
+        ],
+        compiler_params=pltpu.CompilerParams(vmem_limit_bytes=63 * 2**20),
+    )(small, *arrays)
+
+
+def run_layer(tokens, cotangent, segment_ids, inner_bias, vectors, *state):
     n_tok = cotangent.shape[0]
     width = tokens.shape[1]
-    rows = packs.shape[1]
+    rows = state[0].shape[1]
     span = 3 * n_tok // 4
     vmem = pl.BlockSpec(memory_space=pltpu.VMEM)
+    hbm = pl.BlockSpec(memory_space=pl.ANY)
     low = lambda *shape: pltpu.VMEM(shape, BF16)
     wide = lambda *shape: pltpu.VMEM(shape, F32)
     dma = lambda *shape: pltpu.SemaphoreType.DMA(shape)
@@ -876,13 +1223,14 @@
         out_shape=(
             jax.ShapeDtypeStruct((n_tok, width), BF16),
             jax.ShapeDtypeStruct((n_tok, width), F32),
-            jax.ShapeDtypeStruct((3, rows, width), F32),
+            *(jax.ShapeDtypeStruct(v.shape, F32) for v in state),
             jax.ShapeDtypeStruct((16, width), F32),
         ),
-        in_specs=[pl.BlockSpec(memory_space=pl.ANY)] + [vmem] * 5,
-        out_specs=(vmem,) * 4,
+        in_specs=[hbm] * 2 + [vmem] * 3 + [hbm] * 12,
+        out_specs=(hbm,) * 14 + (vmem,),
         scratch_shapes=[
             low(3, PLANES, width, width),
+            low(n_tok, width),
             low(n_tok, width),
             low(2, CHIPS * rows, n_tok),
             low(2, CHIPS * rows, n_tok),
@@ -899,30 +1247,35 @@
             low(n_tok, width),
             wide(PLANES, 8, width),
             wide(2, span, n_tok // 2),
-            low(SLOTS_HELD, 2, CHIPS * rows, width),
+            low(LEAVING, CHIPS * rows, width),
+            low(KEPT + 3, CHIPS * rows, width),
             low(LENT, CHIPS * rows, width),
             low(12, 2, rows // 2, width),
             low(12, 2, rows, width),
             low(3, 3, rows, width),
+            low(3, CHIPS * rows, width),
+            wide(3, rows, width),
             wide(PLANES, 8, width),
             wide(16, width),
             wide(3, 16, width),
             wide(PLANES, 16, width),
-            dma(3, 35),
-            dma(3, 35),
+            *(wide(*state[i].shape) for i in (0, 1, 2, 3, 4, 5, 6, 9)),
+            dma(3, 41),
+            dma(3, 41),
             dma(12, 6),
             dma(12, 6),
             dma(6),
             dma(6),
             dma(3),
             dma(3),
-            pltpu.SemaphoreType.DMA,
+            dma(14),
+            dma(14),
             pltpu.SemaphoreType.REGULAR,
         ],
         compiler_params=pltpu.CompilerParams(
             collective_id=0, has_side_effects=True, vmem_limit_bytes=63 * 2**20
         ),
-    )(tokens, cotangent, segment_ids, packs, bias_rows, vectors)
+    )(tokens, cotangent, segment_ids, inner_bias, vectors, *state)
 
 
 def on_device_whole(
@@ -934,79 +1287,18 @@
     inner_bias, inner_first, inner_second,
     vectors, vector_first, vector_second,
 ):
-    rows, local_width = input_weight.shape[1:]
-    width = tokens.shape[1]
-    local = 3 * DH
-    low = lambda v: v.astype(BF16)
-    pack_a = jnp.concatenate(
-        [
-            low(input_weight[0]), low(input_weight[1]), low(output_weight).T, low(input_weight[2])
-        ],
-        axis=1,
-    )
-    packs = jnp.stack([pack_a, low(up_weight), low(down_weight).T])
-    none = jnp.zeros((local_width,), F32)
-    bias_rows = jnp.concatenate(
-        [
-            jnp.concatenate([inner_bias[0], none, none, inner_bias[1]])[None],
-            inner_bias[2:].T.reshape(1, -1),
-            jnp.zeros((6, width), F32),
-        ],
-        axis=0,
-    )
-    vec_rows = jnp.concatenate([vectors, jnp.zeros((2, width), F32)], axis=0)
-    block_out, token_grad, shard_grads, small = run_layer(
-        tokens, cotangent, segment_ids, packs, bias_rows, vec_rows
-    )
-    input_shard = jnp.stack(
-        [
-            shard_grads[2, :, :local],
-            shard_grads[2, :, local : 2 * local],
-            shard_grads[2, :, 3 * local :],
-        ]
-    )
-    output_shard = shard_grads[2, :, 2 * local : 3 * local].T
-    up_shard = shard_grads[1]
-    down_shard = shard_grads[0].T
-    own = lax.dynamic_slice_in_dim(small, 2 * lax.axis_index("tensor"), 2, 0)
-    inner_grad = jnp.concatenate(
-        [own[0:1, :local], own[0:1, 3 * local :], own[1].reshape(local, 4).T], axis=0
-    )
-    vector_sum = small[8:14]
-    new_input = adam_update(
-        input_weight, input_first, input_second, input_shard, RATE_INPUT, WEIGHT_DECAY
-    )
-    new_output = adam_update(
-        output_weight, output_first, output_second, output_shard, RATE_OUTPUT, WEIGHT_DECAY
-    )
-    new_up = adam_update(up_weight, up_first, up_second, up_shard, RATE_UP, WEIGHT_DECAY)
-    new_down = adam_update(
-        down_weight, down_first, down_second, down_shard, RATE_DOWN, WEIGHT_DECAY
-    )
-    new_inner = adam_update(inner_bias, inner_first, inner_second, inner_grad, RATE_VECTOR, 0.0)
-    new_vector = adam_update(vectors, vector_first, vector_second, vector_sum, RATE_OUTER, 0.0)
-    return (
-        block_out,
-        token_grad,
-        new_input[0],
-        new_input[1],
-        new_input[2],
-        new_output[0],
-        new_output[1],
-        new_output[2],
-        new_up[0],
-        new_up[1],
-        new_up[2],
-        new_down[0],
-        new_down[1],
-        new_down[2],
-        new_inner[0],
-        new_inner[1],
-        new_inner[2],
-        new_vector[0],
-        new_vector[1],
-        new_vector[2],
-    )
+    block_out, token_grad, *state, small = run_layer(
+        tokens, cotangent, segment_ids, inner_bias, vectors,
+        input_weight, input_first, input_second,
+        output_weight, output_first, output_second,
+        up_weight, up_first, up_second,
+        down_weight.T, down_first.T, down_second.T,
+    )
+    results = hand_out(
+        small, inner_bias, inner_first, inner_second, vectors, vector_first, vector_second,
+        block_out, token_grad, *state,
+    )
+    return *results[:11], *(v.T for v in results[11:14]), *results[14:]
 
 
 def solution(mesh):

time: 193 us -> 173 us (0.90)
  other arithmetic: 12.2 us -> 0 us
  local copies, waits for them, and re-layouts: 6.95 us -> 0 us
    sub x6 -> x0, other arithmetic: 7.57 us -> none  [adam_update(): weight - step_rate * (step_ratio + weight_decay * weight)]
    pallas_call x1, Pallas kernels: 173 us -> 166 us  [run_layer(): pl.pallas_call(layer_kernel, name='encoder_layer', out_shape=(jax.ShapeDt...]
    pallas_call x0 -> x1, Pallas kernels: none -> 5.85 us  [hand_out(): pl.pallas_call(hand_out_kernel, name='hand_out', out_shape=(*map(like, mo...]
    unnamed x54 -> x0, local copies, waits for them, and re-layouts: 4.62 us -> none
    another operation x5 -> x0, other arithmetic: 3.9 us -> none  [the longest x4 2.92 us: on_device_whole(): packs = jnp.stack([pack_a, low(up_weight), low(down_weight).T])]
where the time goes in v3:
time: 173 us
  Pallas kernels  172 us (99%)
    pallas_call x1, Pallas kernels, run_layer(): pl.pallas_call(layer_kernel, name='encoder_layer', out_shape=(jax.ShapeDt...  166 us
    pallas_call x1, Pallas kernels, hand_out(): pl.pallas_call(hand_out_kernel, name='hand_out', out_shape=(*map(like, mo...  5.85 us

profile of v3, /device:TPU:0, one launch (start us, length us, event | category | flops | bytes accessed | tf_op | source)
XLA Modules:
  0.0 172.8 jit_solution(6448272220377416521)
XLA Ops:
  0.7 166.1 %encoder_layer.1 = (bf16[512,768]{1,0:T(8,128)(2,1)}, f32[512,768]{1,0:T(8,128)}, f32[3,96,192]{2,1,0:T(8,128)}, f32[3,96,192]{2,1,0:T(8,128)}, f32[3,96,192]{2,...) custom-call(bf16[2048,768]{1,0:T(8,128)(2,1)} %tokens_hbm.1, ...), custom_call_target="tpu_custom_call" | custom-call | tf_op jit(solution)/shard_map/encoder_layer/pallas_call | solution.py:1220
  166.8 5.8 %hand_out.1 = (bf16[512,768]{1,0:T(8,128)(2,1)}, f32[512,768]{1,0:T(8,128)}, f32[3,96,192]{2,1,0:T(8,128)}, f32[3,96,192]{2,1,0:T(8,128)}, f32[3,96,192]{2,1,0:T...) custom-call(f32[16,768]{1,0:T(8,128)} %get-tuple-element.55.small_re, ...), custom_call_target="tpu_custom_call" | custom-call | tf_op jit(solution)/shard_map/hand_out/pallas_call | solution.py:1195

commit v4 on v3

--- a/solution.py
+++ b/solution.py
@@ -426,8 +426,7 @@
 
     def handed(m, at, k):
         near = ((k == 1) & (at < PLANES - 1)) | ((k == 3) & (at > 0))
-        edge = (at == 0) | (at == PLANES - 1)
-        return near & ((m == 2) | ((m == 1) & edge))
+        return near & (m == 2)
 
     def pass_on(m, j, which, act):
         @pl.when((z < PLANES - 1) & handed(m, z + 1, 3))
@@ -518,9 +517,9 @@
 
     def gather_calls(i):
         def start_next():
-            @pl.when(i < 9)
+            @pl.when(i < 10)
             def _():
-                first(*place(i + 3))
+                first(*place(i + 2))
 
         def middle():
             @pl.when(i < 11)
@@ -528,20 +527,19 @@
                 second(*place(i + 1))
 
         def last():
+            @pl.when(i < 12)
+            def _():
+                third(*place(i))
+
+        def whole():
             @pl.when((i > 0) & (i <= 12))
             def _():
-                third(*place(i - 1))
-
-        def whole():
-            @pl.when((i > 1) & (i <= 13))
-            def _():
-                fourth(*place(i - 2))
+                fourth(*place(i - 1))
 
         return start_next, middle, last, whole
 
     first(0, 0)
     first(1, 0)
-    first(2, 0)
     spread = lax.broadcasted_iota(jnp.int32, (local, width), 1) - PLANES * lax.broadcasted_iota(
         jnp.int32, (local, width), 0
     )
@@ -591,7 +589,7 @@
     lane = lax.broadcasted_iota(jnp.int32, (1, width), 1)
     q_scale = jnp.where(lane < 3 * DH, 1.0 / math.sqrt(DH), 1.0)
     heads = 3
-    for i in range(3):
+    for i in range(2):
         for call in gather_calls(i):
             call()
 
@@ -677,9 +675,9 @@
 
         @pl.loop(0, PLANES)
         def _(k, p=p, work=work):
-            calls = gather_calls(jnp.where(k < 3, 3 * p + k + 5, 99))
+            calls = gather_calls(PLANES * p + k + 3 if p else jnp.where(k < 3, k + 4, 99))
             if p == 0:
-                calls = tuple(early(k, i) for i in (3, 4)) + calls
+                calls = tuple(early(k, i) for i in (2, 3)) + calls
             weave(work(k), calls)
 
         if p == 0:
@@ -758,9 +756,8 @@
         return red(kept(p, kk, chip), ZR.at[p, kk], p, kk, 5, (dp, (z + 1 + kk) & (PLANES - 1)))
 
     def all_along_z(p, kk):
-        side = jnp.where(p == 0, kk >> 1, 2)
         return red(
-            OWN.at[spot(p, kk)], PZ.at[side], p, kk, 5, (dp, (z + 1 + kk) & (PLANES - 1))
+            OWN.at[spot(p, kk)], PZ.at[kk >> 1], p, kk, 5, (dp, (z + 1 + kk) & (PLANES - 1))
         )
 
     def step_one(u):
@@ -788,7 +785,7 @@
 
         @pl.when((kk == PLANES - 1) & there & handed(2 - p, at_z, at_k))
         def _():
-            side = jnp.where(p == 0, (at_k - 1) // 2, 2)
+            side = at_k >> 1
             red(PZ.at[0], PZ.at[0], p, at_k - 1, 5, dev_sib).wait_recv()
             for j in range(CHIPS):
                 at, here, total = add_to(p, kk, j, [PZ[side, unit_rows(j), :]])
@@ -856,40 +853,53 @@
             def _():
                 along_z(p, kk).wait_send()
 
-    def item(i):
-        p = third_of(i)
-        kk = i - 3 * p
-        late = (i == 6) | (i >= 10)
-        p = jnp.where(i == 6, 0, jnp.where(i == 10, 1, jnp.where(i > 6, 2, p)))
-        kk = jnp.where(late, PLANES - 1, jnp.where(i > 6, i - 7, kk))
-        return p, kk
-
-    def reduce_calls(u):
+    travel = ((0, 0), (0, 1), (0, 2), (1, 0), (1, 1), (1, 2), (0, 3), (2, 0), (2, 1), (2, 2), (1, 3), (2, 3))
+    no = len(travel)
+
+    def pick(k, values):
+        chosen = values[0]
+        for at in range(1, len(values)):
+            chosen = jnp.where(k == at, values[at], chosen)
+        return chosen
+
+    def stage(step, k, items):
+        known = [travel[i % no] for i in items]
+
+        def call():
+            @pl.when(pick(k, [int(i != no) for i in items]) == 1)
+            def _():
+                step(pick(k, [p for p, _ in known]), pick(k, [kk for _, kk in known]))
+
+        return call
+
+    def reduce_calls(p, k):
+        u = PLANES * p + k
+
         def merge():
-            @pl.when((u >= 1) & (u < 13))
+            @pl.when(u >= 1)
             def _():
                 step_two(u - 1)
 
-        def stage(lag, step):
-            i = u - lag
-            i = jnp.where(i >= 3, i - 1, i)
-
-            def call():
-                @pl.when((u >= lag) & (u != lag + 3) & (i < 12))
-                def _():
-                    step(*item(i))
-
-            return call
-
         def merge_and_relay():
             merge()
-            stage(1, step_three)()
-
-        return stage(3, step_four), stage(4, step_five), merge_and_relay
-
-    def reduce_step(u):
-        for call in reduce_calls(u):
-            call()
+            stage(step_three, k, ((no, 0, 1, 2), (no, 3, 4, 5), (6, 7, 8, 9))[p])()
+
+        if p == 0:
+            return stage(step_four, k, (no, no, no, 0)), merge_and_relay
+        if p == 1:
+            return (
+                stage(step_four, k, (1, 2, no, 3)),
+                merge_and_relay,
+                stage(step_five, k, (no, 0, 1, 2)),
+            )
+        return (
+            stage(step_four, k, (4, 6, 7, 8)),
+            merge_and_relay,
+            stage(step_five, k, (no, 3, 5, 6)),
+            stage(step_four, k, (5, no, no, no)),
+            stage(step_five, k, (no, 4, no, no)),
+            stage(step_three, k, (no, no, no, 10)),
+        )
 
     def before_unit(u):
         p, kk = u >> 2, u & 3
@@ -1051,7 +1061,7 @@
         def _(kk, p=p, work=work):
             u = p * PLANES + kk
             before_unit(u)
-            weave(work(u, (kk + 1) & 3), reduce_calls(u))
+            weave(work(u, (kk + 1) & 3), reduce_calls(p, kk))
 
         if p == 0:
             transposed(NB, XT)
@@ -1072,29 +1082,41 @@
     def small(step, dev):
         return remote(SMS, SMR.at[step], small_send.at[step], small_recv.at[step], dev)
 
-    for step, dev in enumerate((dev_sib, dev_x, dev_y)):
-        reduce_step(12 + step)
-        copy = small(step, dev)
-        copy.start()
-        copy.wait()
+    small_copies = [small(step, dev) for step, dev in enumerate((dev_sib, dev_x, dev_y))]
+
+    def small_sum(step):
+        small_copies[step].wait()
         SMS[...] += SMR[step]
-
-    SMZ[z] = SMS[...]
 
     def small_z(k, dev):
         return remote(SMS, SMZ.at[z], small_send.at[2 + k], small_recv.at[2 + k], dev)
 
+    small_copies[0].start()
+    step_two(11)
+    step_three(*travel[11])
+    step_four(*travel[9])
+    step_five(*travel[7])
+    small_sum(0)
+    small_copies[1].start()
+    step_four(*travel[10])
+    step_five(*travel[8])
+    small_sum(1)
+    small_copies[2].start()
+    step_four(*travel[11])
+    step_five(*travel[9])
+    small_sum(2)
+    SMZ[z] = SMS[...]
     for k in (1, 2, 3):
         small_z(k, dev_z(PLANES - k)).start()
+    step_five(*travel[10])
+    finish(1)
+    step_five(*travel[11])
     for k in (1, 2, 3):
         remote(
             SMS, SMZ.at[plane(k)], small_send.at[2 + k], small_recv.at[2 + k], dev_sib
         ).wait_recv()
     small_ref[...] = (SMZ[0] + SMZ[1]) + (SMZ[2] + SMZ[3])
 
-    reduce_step(15)
-    finish(1)
-    reduce_step(16)
     finish(2)
 
     for k in (1, 2, 3):
@@ -1253,7 +1275,7 @@
             low(12, 2, rows // 2, width),
             low(12, 2, rows, width),
             low(3, 3, rows, width),
-            low(3, CHIPS * rows, width),
+            low(2, CHIPS * rows, width),
             wide(3, rows, width),
             wide(PLANES, 8, width),
             wide(16, width),

time: 173 us -> 163 us (0.942)
  Pallas kernels: 172 us -> 162 us
    pallas_call x1, Pallas kernels: 166 us -> 156 us  [run_layer(): pl.pallas_call(layer_kernel, name='encoder_layer', out_shape=(jax.ShapeDt...]
where the time goes in v4:
time: 163 us
  Pallas kernels  162 us (99%)
    pallas_call x1, Pallas kernels, run_layer(): pl.pallas_call(layer_kernel, name='encoder_layer', out_shape=(jax.ShapeDt...  156 us
    pallas_call x1, Pallas kernels, hand_out(): pl.pallas_call(hand_out_kernel, name='hand_out', out_shape=(*map(like, mo...  5.85 us

profile of v4, /device:TPU:0, one launch (start us, length us, event | category | flops | bytes accessed | tf_op | source)
XLA Modules:
  0.0 162.6 jit_solution(9667439921594389260)
XLA Ops:
  0.7 155.9 %encoder_layer.1 = (bf16[512,768]{1,0:T(8,128)(2,1)}, f32[512,768]{1,0:T(8,128)}, f32[3,96,192]{2,1,0:T(8,128)}, f32[3,96,192]{2,1,0:T(8,128)}, f32[3,96,192]{2,...) custom-call(bf16[2048,768]{1,0:T(8,128)(2,1)} %tokens_hbm.1, ...), custom_call_target="tpu_custom_call" | custom-call | tf_op jit(solution)/shard_map/encoder_layer/pallas_call | solution.py:1242
  156.6 5.8 %hand_out.1 = (bf16[512,768]{1,0:T(8,128)(2,1)}, f32[512,768]{1,0:T(8,128)}, f32[3,96,192]{2,1,0:T(8,128)}, f32[3,96,192]{2,1,0:T(8,128)}, f32[3,96,192]{2,1,0:T...) custom-call(f32[16,768]{1,0:T(8,128)} %get-tuple-element.55.small_re, ...), custom_call_target="tpu_custom_call" | custom-call | tf_op jit(solution)/shard_map/hand_out/pallas_call | solution.py:1217

commit v5 on v4

--- a/solution.py
+++ b/solution.py
@@ -341,7 +341,7 @@
     block_hbm, tgrad_hbm,
     iw_out, im_out, iv_out, ow_out, om_out, ov_out, uw_out, um_out, uv_out, dw_out, dm_out, dv_out,
     small_ref,
-    W, TOK, COT, XT, XT2, QKV, ATT, PT, PRE, RSTD, NB, PO, HID, GP, GB, DHP,
+    W, TOK, COT, XT_LATE, XT_TOK, XT_NORM, QKV, ATT, PT, PRE, RSTD, NB, PO, HID, GP, GB, DHP,
     BIAS, MASK, OUT, OWN, SR, DR, PR, ZR, PZ, GRAD, SMK, SMS, SMR, SMZ,
     IW, IM, IV, OW, OM, OV, UW, DW,
     gather_send, gather_recv, red_send, red_recv, small_send, small_recv, bias_send, bias_recv,
@@ -406,10 +406,6 @@
     W[0, z, rd(chip, core), :] = jnp.concatenate(
         [IW[0], IW[1], OW[...].T, IW[2]], axis=1
     ).astype(BF16)
-    loads[2].wait()
-    W[1, z, rd(chip, core), :] = UW[...].astype(BF16)
-    loads[3].wait()
-    W[2, z, rd(chip, core), :] = DW[...].astype(BF16)
     pl.semaphore_wait(barrier, 6)
 
     def send_block(m, t, j, c, kind, dev, start=0, size=rows):
@@ -426,7 +422,8 @@
 
     def handed(m, at, k):
         near = ((k == 1) & (at < PLANES - 1)) | ((k == 3) & (at > 0))
-        return near & (m == 2)
+        edge = (at == 0) | (at == PLANES - 1)
+        return near & ((m == 2) | ((m == 1) & edge))
 
     def pass_on(m, j, which, act):
         @pl.when((z < PLANES - 1) & handed(m, z + 1, 3))
@@ -510,21 +507,37 @@
     def third_of(i):
         return (i * 11) >> 5
 
+    def pick(k, values):
+        chosen = values[0]
+        for at in range(1, len(values)):
+            chosen = jnp.where(k == at, values[at], chosen)
+        return chosen
+
+    journey = (
+        (0, 0), (1, 0), (0, 1), (0, 2), (0, 3), (2, 0), (1, 1), (1, 2), (1, 3), (2, 2), (2, 1), (2, 3)
+    )
+
     def place(i):
-        later = (i >= 3).astype(jnp.int32) if not isinstance(i, int) else int(i >= 3)
-        m = i - later * (i - third_of(i - 3))
-        return m, later * (i - 2 - 3 * m)
+        if isinstance(i, int):
+            return journey[i]
+        return pick(i, [m for m, _ in journey]), pick(i, [k for _, k in journey])
+
+    def pause():
+        pass
 
     def gather_calls(i):
         def start_next():
-            @pl.when(i < 10)
-            def _():
-                first(*place(i + 2))
-
-        def middle():
             @pl.when(i < 11)
             def _():
                 second(*place(i + 1))
+
+            @pl.when(i < 9)
+            def _():
+                first(*place(i + 3))
+
+            @pl.when(i == 2)
+            def _():
+                z_sends(2)
 
         def last():
             @pl.when(i < 12)
@@ -536,9 +549,11 @@
             def _():
                 fourth(*place(i - 1))
 
-        return start_next, middle, last, whole
+        return start_next, pause, last, whole
 
     first(0, 0)
+    loads[2].wait()
+    W[1, z, rd(chip, core), :] = UW[...].astype(BF16)
     first(1, 0)
     spread = lax.broadcasted_iota(jnp.int32, (local, width), 1) - PLANES * lax.broadcasted_iota(
         jnp.int32, (local, width), 0
@@ -562,9 +577,17 @@
         ).start()
     z_sends(0)
     z_sends(1)
-    z_sends(2)
+    loads[3].wait()
+    W[2, z, rd(chip, core), :] = DW[...].astype(BF16)
     tok_copy.wait()
     second(0, 0)
+    first(*place(2))
+
+    def transposed(src, dst):
+        for j in range(CHIPS):
+            for c in range(2):
+                lo = (2 * j + c) * rows
+                dst[c, j * rows : (j + 1) * rows, :] = src[:, lo : lo + rows].T
 
     vec = vec_ref[...]
 
@@ -573,6 +596,7 @@
         part = pl.ds(pl.multiple_of(r * (n_tok // 8), 16), n_tok // 8)
         PRE[part, :] = TOK[part, :].astype(F32) + vec[0:1]
 
+    transposed(TOK, XT_TOK)
     seg_row = seg_ref[pl.ds(z, 1), :].astype(F32)
     seg_col = jnp.broadcast_to(seg_row, (128, n_tok)).T
     span = 3 * n_tok // 4
@@ -633,7 +657,7 @@
             PRE[:, cols] += mm_nt(out, W[0, t, cols, 2 * local : 3 * local])
 
     def forward_norm():
-        @pl.loop(0, 8)
+        @pl.loop(0, 8, unroll=2)
         def _(r):
             part = pl.ds(pl.multiple_of(r * (n_tok // 8), 16), n_tok // 8)
             rows_in = PRE[part, :]
@@ -675,20 +699,21 @@
 
         @pl.loop(0, PLANES)
         def _(k, p=p, work=work):
-            calls = gather_calls(PLANES * p + k + 3 if p else jnp.where(k < 3, k + 4, 99))
+            calls = gather_calls(PLANES * p + k + 3)
             if p == 0:
-                calls = tuple(early(k, i) for i in (2, 3)) + calls
-            weave(work(k), calls)
+                calls = (early(k, 2), *calls)
+            weave(work(((k & 1) << 1) | (k >> 1) if p == 2 else k), calls)
 
         if p == 0:
             forward_norm()
+            transposed(NB, XT_NORM)
 
     cot_copy.wait()
 
     SMK[...] = jnp.zeros_like(SMK)
     SMS[...] = jnp.zeros_like(SMS)
 
-    @pl.loop(0, 8)
+    @pl.loop(0, 8, unroll=2)
     def _(r):
         part = pl.ds(pl.multiple_of(r * (n_tok // 8), 16), n_tok // 8)
         rows_in = PO[part, :]
@@ -757,7 +782,7 @@
 
     def all_along_z(p, kk):
         return red(
-            OWN.at[spot(p, kk)], PZ.at[kk >> 1], p, kk, 5, (dp, (z + 1 + kk) & (PLANES - 1))
+            OWN.at[spot(p, kk)], PZ.at[jnp.where(p == 0, kk >> 1, 2)], p, kk, 5, (dp, (z + 1 + kk) & (PLANES - 1))
         )
 
     def step_one(u):
@@ -771,8 +796,7 @@
         to_sibling(u).wait_recv()
         p, kk = u >> 2, u & 3
         for j in range(CHIPS):
-            at, here, total = add_to(p, kk, j, [SR[u & (LENT - 1), unit_rows(j), :]])
-            OWN[at, here, :] = total.astype(BF16)
+            OWN[spot(p, kk), unit_rows(j), :] += SR[u & (LENT - 1), unit_rows(j), :]
 
         @pl.when(u < 12 - LENT)
         def _():
@@ -785,11 +809,10 @@
 
         @pl.when((kk == PLANES - 1) & there & handed(2 - p, at_z, at_k))
         def _():
-            side = at_k >> 1
+            side = jnp.where(p == 0, at_k >> 1, 2)
             red(PZ.at[0], PZ.at[0], p, at_k - 1, 5, dev_sib).wait_recv()
             for j in range(CHIPS):
-                at, here, total = add_to(p, kk, j, [PZ[side, unit_rows(j), :]])
-                OWN[at, here, :] = total.astype(BF16)
+                OWN[spot(p, kk), unit_rows(j), :] += PZ[side, unit_rows(j), :]
 
     def step_three(p, kk):
         take_handed(p, kk, True)
@@ -810,12 +833,10 @@
         def _():
             u = 4 * p + kk
             relay_y(p, kk).wait_recv()
-            at, here, total = add_to(p, kk, jx, [DR[u, 0]], 0, half)
-            OWN[at, here, :] = total.astype(BF16)
+            OWN[spot(p, kk), unit_rows(jx, 0, half), :] += DR[u, 0]
             along_x(p, kk).start()
             relay_x(p, kk).wait_recv()
-            at, here, total = add_to(p, kk, jy, [DR[u, 1]], half, half)
-            OWN[at, here, :] = total.astype(BF16)
+            OWN[spot(p, kk), unit_rows(jy, half, half), :] += DR[u, 1]
             along_y(p, kk).start()
 
     def step_five(p, kk):
@@ -855,12 +876,6 @@
 
     travel = ((0, 0), (0, 1), (0, 2), (1, 0), (1, 1), (1, 2), (0, 3), (2, 0), (2, 1), (2, 2), (1, 3), (2, 3))
     no = len(travel)
-
-    def pick(k, values):
-        chosen = values[0]
-        for at in range(1, len(values)):
-            chosen = jnp.where(k == at, values[at], chosen)
-        return chosen
 
     def stage(step, k, items):
         known = [travel[i % no] for i in items]
@@ -890,10 +905,12 @@
             return (
                 stage(step_four, k, (1, 2, no, 3)),
                 merge_and_relay,
+                pause,
                 stage(step_five, k, (no, 0, 1, 2)),
             )
         return (
             stage(step_four, k, (4, 6, 7, 8)),
+            pause,
             merge_and_relay,
             stage(step_five, k, (no, 3, 5, 6)),
             stage(step_four, k, (5, no, no, no)),
@@ -913,24 +930,24 @@
         def _():
             to_sibling(u - LEAVING).wait_send()
 
-    def transposed(src, dst):
-        for j in range(CHIPS):
-            for c in range(2):
-                lo = (2 * j + c) * rows
-                dst[c, j * rows : (j + 1) * rows, :] = src[:, lo : lo + rows].T
-
-    def fill(u, left, right_of, lo, hi):
-        OUT[u & (LEAVING - 1), :, lo:hi] = mm(left[1 - core], right_of(lo, hi)).astype(BF16)
-        OWN[spot(u >> 2, u & 3), :, lo:hi] = mm(left[core], right_of(lo, hi)).astype(BF16)
-
-    transposed(GB, XT)
+    def fill_out(u, left, right, lo, hi):
+        OUT[u & (LEAVING - 1), :, lo:hi] = mm(left[1 - core], right).astype(BF16)
+
+    def fill_own(u, left, right, lo, hi):
+        OWN[spot(u >> 2, u & 3), :, lo:hi] = mm(left[core], right).astype(BF16)
+
+    thirds = tuple((n * TILE, (n + 1) * TILE) for n in range(3))
+
+    transposed(GB, XT_LATE)
 
     def backward_down(u, k):
+        for lo, hi in thirds:
+            fill_out(u, XT_LATE, HID[k, :, lo:hi], lo, hi)
+        step_one(u)
         yield
-        for n in range(3):
-            fill(u, XT, lambda lo, hi: HID[k, :, lo:hi], n * TILE, (n + 1) * TILE)
+        for lo, hi in thirds:
+            fill_own(u, XT_LATE, HID[k, :, lo:hi], lo, hi)
             yield
-        step_one(u)
 
     def backward_up(u, k):
         t = plane(k)
@@ -942,9 +959,11 @@
             DHP[:, cols] = low
             SMK[t, 1:2, cols] = jnp.sum(low.astype(F32), axis=0, keepdims=True)
         yield
-        for n in range(3):
-            fill(u, XT, lambda lo, hi: DHP[:, lo:hi], n * TILE, (n + 1) * TILE)
+        for lo, hi in thirds:
+            fill_out(u, XT_NORM, DHP[:, lo:hi], lo, hi)
         step_one(u)
+        for lo, hi in thirds:
+            fill_own(u, XT_NORM, DHP[:, lo:hi], lo, hi)
         yield
         for n in range(3):
             cols = slice(n * TILE, (n + 1) * TILE)
@@ -952,7 +971,7 @@
         yield
 
     def backward_norm():
-        @pl.loop(0, 8)
+        @pl.loop(0, 8, unroll=2)
         def _(r):
             part = pl.ds(pl.multiple_of(r * (n_tok // 8), 16), n_tok // 8)
             grad_in = PO[part, :]
@@ -1006,10 +1025,12 @@
             grads[0] + grads[1] + [empty] + grads[2], axis=1
         ).astype(BF16)
         SMK[t, 0:1, :] = jnp.sum(DHP[...].astype(F32), axis=0, keepdims=True)
-        fill(u, XT, lambda lo, hi: DHP[:, lo:hi], 0, 2 * local)
-        fill(u, XT2, lambda lo, hi: ATT[k], 2 * local, 3 * local)
-        fill(u, XT, lambda lo, hi: DHP[:, lo:hi], 3 * local, 4 * local)
-        step_one(u)
+        for fill in (fill_out, fill_own):
+            fill(u, XT_TOK, DHP[:, : 2 * local], 0, 2 * local)
+            fill(u, XT_LATE, ATT[k], 2 * local, 3 * local)
+            fill(u, XT_TOK, DHP[:, 3 * local :], 3 * local, 4 * local)
+            if fill is fill_out:
+                step_one(u)
         yield
         for n in range(3):
             cols = slice(n * TILE, (n + 1) * TILE)
@@ -1063,14 +1084,11 @@
             before_unit(u)
             weave(work(u, (kk + 1) & 3), reduce_calls(p, kk))
 
-        if p == 0:
-            transposed(NB, XT)
         if p == 1:
             backward_norm()
             for copy in loads[8:]:
                 copy.start()
-            transposed(TOK, XT)
-            transposed(GB, XT2)
+            transposed(GB, XT_LATE)
         if p == 2:
             finish(0)
 
@@ -1162,21 +1180,24 @@
         copy.wait()
 
 
-def hand_out_kernel(small_ref, iw, im, iv, vw, vm, vv, *refs):
-    moved = (len(refs) - 8) // 3
-    sources, targets = refs[:moved], refs[moved : 2 * moved]
-    iw_out, im_out, iv_out, vw_out, vm_out, vv_out = refs[2 * moved : 2 * moved + 6]
-    staged, sem = refs[2 * moved + 6 : -2], refs[-2:]
+def hand_out_kernel(*refs):
+    moved = (len(refs) - 7) // 3
+    sources, targets = refs[:moved], refs[moved : 2 * moved - 1]
+    staged, new = refs[2 * moved - 1 : 3 * moved - 1], refs[3 * moved - 1 : -2]
+    load_sem, store_sem = refs[-2:]
     loads = [
-        pltpu.make_async_copy(src, mid, sem[0].at[i])
+        pltpu.make_async_copy(src, mid, load_sem.at[i])
         for i, (src, mid) in enumerate(zip(sources, staged))
     ]
     stores = [
-        pltpu.make_async_copy(mid, dst, sem[1].at[i])
-        for i, (mid, dst) in enumerate(zip(staged, targets))
+        pltpu.make_async_copy(mid, dst, store_sem.at[i])
+        for i, (mid, dst) in enumerate(zip((*new, *staged[7:]), targets))
     ]
     for copy in loads:
         copy.start()
+    for copy in loads[:7]:
+        copy.wait()
+    small_ref, iw, im, iv, vw, vm, vv = staged[:7]
     z = lax.axis_index("tensor")
     small = small_ref[...]
     width = small.shape[1]
@@ -1197,36 +1218,37 @@
         )
         for r in range(4)
     ]
-    for load, store in zip(loads, stores):
+    for load, store in zip(loads[7:], stores[6:]):
         load.wait()
         store.start()
     inner_grad = jnp.concatenate([own[:, :local], own[:, 3 * local :], *picked], axis=0)
-    new = adam_update(iw[...], im[...], iv[...], inner_grad, RATE_VECTOR, 0.0)
-    iw_out[...], im_out[...], iv_out[...] = new
-    new = adam_update(vw[...], vm[...], vv[...], small[8:14], RATE_OUTER, 0.0)
-    vw_out[...], vm_out[...], vv_out[...] = new
+    updated = (
+        *adam_update(iw[...], im[...], iv[...], inner_grad, RATE_VECTOR, 0.0),
+        *adam_update(vw[...], vm[...], vv[...], small[8:14], RATE_OUTER, 0.0),
+    )
+    for ref, value, store in zip(new, updated, stores):
+        ref[...] = value
+        store.start()
     for store in stores:
         store.wait()
 
 
-def hand_out(small, *arrays):
-    params, moved = arrays[:6], arrays[6:]
-    vmem = pl.BlockSpec(memory_space=pltpu.VMEM)
+def hand_out(*arrays):
     hbm = pl.BlockSpec(memory_space=pl.ANY)
-    like = lambda v: jax.ShapeDtypeStruct(v.shape, v.dtype)
     return pl.pallas_call(
         hand_out_kernel,
         name="hand_out",
-        out_shape=(*map(like, moved), *map(like, params)),
-        in_specs=[vmem] * 7 + [hbm] * len(moved),
-        out_specs=(hbm,) * len(moved) + (vmem,) * 6,
+        out_shape=tuple(jax.ShapeDtypeStruct(v.shape, v.dtype) for v in arrays[1:]),
+        in_specs=[hbm] * len(arrays),
+        out_specs=(hbm,) * (len(arrays) - 1),
         scratch_shapes=[
-            *(pltpu.VMEM(v.shape, v.dtype) for v in moved),
-            pltpu.SemaphoreType.DMA((len(moved),)),
-            pltpu.SemaphoreType.DMA((len(moved),)),
+            *(pltpu.VMEM(v.shape, v.dtype) for v in arrays),
+            *(pltpu.VMEM(v.shape, v.dtype) for v in arrays[1:7]),
+            pltpu.SemaphoreType.DMA((len(arrays),)),
+            pltpu.SemaphoreType.DMA((len(arrays) - 1,)),
         ],
         compiler_params=pltpu.CompilerParams(vmem_limit_bytes=63 * 2**20),
-    )(small, *arrays)
+    )(*arrays)
 
 
 def run_layer(tokens, cotangent, segment_ids, inner_bias, vectors, *state):
@@ -1256,6 +1278,7 @@
             low(n_tok, width),
             low(2, CHIPS * rows, n_tok),
             low(2, CHIPS * rows, n_tok),
+            low(2, CHIPS * rows, n_tok),
             low(PLANES, n_tok, width),
             low(PLANES, n_tok, 3 * DH),
             low(PLANES, 3, 2, span, n_tok // 2),
@@ -1275,7 +1298,7 @@
             low(12, 2, rows // 2, width),
             low(12, 2, rows, width),
             low(3, 3, rows, width),
-            low(2, CHIPS * rows, width),
+            low(3, CHIPS * rows, width),
             wide(3, rows, width),
             wide(PLANES, 8, width),
             wide(16, width),
@@ -1320,7 +1343,8 @@
         small, inner_bias, inner_first, inner_second, vectors, vector_first, vector_second,
         block_out, token_grad, *state,
     )
-    return *results[:11], *(v.T for v in results[11:14]), *results[14:]
+    small_results, results = results[:6], results[6:]
+    return *results[:11], *(v.T for v in results[11:]), *small_results
 
 
 def solution(mesh):

time: 163 us -> 151 us (0.926)
  Pallas kernels: 162 us -> 150 us
    pallas_call x1, Pallas kernels: 156 us -> 145 us  [run_layer(): pl.pallas_call(layer_kernel, name='encoder_layer', out_shape=(jax.ShapeDt...]
where the time goes in v5:
time: 151 us
  Pallas kernels  150 us (99%)
    pallas_call x1, Pallas kernels, run_layer(): pl.pallas_call(layer_kernel, name='encoder_layer', out_shape=(jax.ShapeDt...  145 us
    pallas_call x1, Pallas kernels, hand_out(): pl.pallas_call(hand_out_kernel, name='hand_out', out_shape=tuple((jax.Sha...  5.32 us

profile of v5, /device:TPU:0, one launch (start us, length us, event | category | flops | bytes accessed | tf_op | source)
XLA Modules:
  0.0 151.1 jit_solution(3821799521846512864)
XLA Ops:
  0.7 144.9 %encoder_layer.1 = (bf16[512,768]{1,0:T(8,128)(2,1)}, f32[512,768]{1,0:T(8,128)}, f32[3,96,192]{2,1,0:T(8,128)}, f32[3,96,192]{2,1,0:T(8,128)}, f32[3,96,192]{2,...) custom-call(bf16[2048,768]{1,0:T(8,128)(2,1)} %tokens_hbm.1, ...), custom_call_target="tpu_custom_call" | custom-call | tf_op jit(solution)/shard_map/encoder_layer/pallas_call | solution.py:1264
  145.6 5.3 %hand_out.1 = (f32[6,192]{1,0:T(8,128)}, f32[6,192]{1,0:T(8,128)}, f32[6,192]{1,0:T(8,128)}, f32[6,768]{1,0:T(8,128)}, f32[6,768]{1,0:T(8,128)}, /*index=5*/f32[...) custom-call(f32[16,768]{1,0:T(8,128)} %get-tuple-element.55.refs_0_,, ...), custom_call_target="tpu_custom_call" | custom-call | tf_op jit(solution)/shard_map/hand_out/pallas_call | solution.py:1238
